TPU v7x, 128 devices: a whole 4x4x4 slice. The times are simulated.
128 devices in a mesh: tm: 32 (over y, x, core), zone: 4 (over z).
Axes of the slice: x: 4, y: 4, z: 4, core: 2. Of those that a mesh axis runs over, the one named last changes fastest.
Arguments:
- gains: float32 [8192, 128, 128], P(('tm', 'zone')), may hold values from -1 to 1, as said below
- means: float32 [8192, 128], P(('tm', 'zone')), may hold values from -0.4 to 0.4
- transition: float32 [128, 128], replicated, may hold values from -0.25 to 0.25
- observations: bfloat16 [8192, 98304], P('tm', 'zone'), may hold values from -6 to 6
- loadings: bfloat16 [98304, 128], P('zone'), may hold values from -0.5 to 0.5
Outputs:
- smoothed: float32 [8192, 128], P(('tm', 'zone'))
- load_grad: float32 [98304, 128], P(('zone', 'tm'))
Inputs may be any that keep to these rules, and one draw needn't show every extreme that they name: `gains`: one 128 x 128 gain matrix a time step.
All inputs are finite; a program needn't handle non-finite values.
Results may differ from a plain program's by a relative error of at most 0.0009.
Values may be sent and summed in bfloat16 or wider, within the bound.
No kernel may reach another device: no remote copies, remote signals or barrier semaphores. Data moves between devices by JAX's collectives and lax.ppermute only.
A program may use at most 192 MiB of HBM per device.

v0:
```python
import jax
import jax.numpy as jnp
from jax import lax
from jax.experimental import pallas as pl
from jax.experimental.pallas import tpu as pltpu
from jax.sharding import PartitionSpec as P

K = 128
AUG = 136
CHUNK = 8
SIDE = 4
WIDTH = 768
FAR_MIB, SIDE_MIB, STEP_MIB, OWN_MIB = 52, 50, 48, 46
HALF = 384
TM = (4, 4, 2)
Y, X, CORE = 0, 1, 2
FULL = lax.Precision.HIGHEST
F32 = jnp.float32
BF16 = jnp.bfloat16
NT = (((1,), (1,)), ((), ()))
NN = (((1,), (0,)), ((), ()))
VM = pl.BlockSpec(memory_space=pltpu.VMEM)
SM = pl.BlockSpec(memory_space=pltpu.SMEM)
HBM = pl.BlockSpec(memory_space=pltpu.HBM)


def params(mib):
    return pltpu.CompilerParams(vmem_limit_bytes=mib << 20)


def thirds(x):
    a = x.astype(BF16)
    x = x - a.astype(F32)
    b = x.astype(BF16)
    return a, b, (x - b.astype(F32)).astype(BF16)


def dot32(a, b, dims):
    a0, a1, a2 = thirds(a)
    b0, b1, b2 = thirds(b)
    at = dims[0][1][0]

    def two(p, q):
        left, right = jnp.concatenate(p, axis=1), jnp.concatenate(q, axis=at)
        return lax.dot_general(left, right, dims, preferred_element_type=F32)

    return two((a0, a1), (b0, b0)) + (two((a0, a1), (b1, b1)) + two((a0, a2), (b2, b0)))


def place(position):
    return position // 32, position // 8 % 4, position // 4 % 2, position % 4


def first_row(row):
    at = lax.broadcasted_iota(jnp.int32, (8, K), 0)
    return jnp.where(at == 0, jnp.broadcast_to(row, (8, K)), 0.0)


def identity_map():
    at = lax.broadcasted_iota(jnp.int32, (AUG, K), 0)
    to = lax.broadcasted_iota(jnp.int32, (AUG, K), 1)
    return jnp.where(at == to, 1.0, 0.0).astype(F32)


def then(late, early):
    out = dot32(late, early[:K], NN)
    return out + jnp.concatenate([jnp.zeros((K, K), F32), early[K:]], axis=0)


def local_kernel(last, at, g, obs, rows_in, maps, tails, shifted, whole, theirs, buf, isem, osem):
    steps = g.shape[0]
    chunks = steps // CHUNK
    units = buf.shape[0]
    _, _, core, _ = place(at[0])

    def obs_in(u):
        col = pl.multiple_of((2 * u + 1 - core) * WIDTH, WIDTH)
        return pltpu.make_async_copy(obs.at[:, pl.ds(col, WIDTH)], buf.at[u], isem.at[u])

    def obs_out(u):
        return pltpu.make_async_copy(buf.at[u], theirs.at[u], osem.at[u])

    def pass_on(u):
        obs_in(u).wait()
        obs_out(u).start()

    for u in range(units):
        obs_in(u).start()

    m = rows_in[0:steps, :]
    p = lax.dot_general(m, rows_in[steps:, :], NT, precision=FULL, preferred_element_type=F32)
    sh = jnp.concatenate([jnp.zeros((1, K), F32), p[: steps - 1]], axis=0)
    shifted[...] = sh
    whole[0:steps, :] = m - sh
    enter = jnp.where(at[0] == last, 0.0, -p[steps - 1 : steps])

    top = CHUNK - 1
    for c in range(chunks):
        t = CHUNK * c + top
        gain = g[t]
        maps[t, 0:K, :] = gain.T
        row = first_row(whole[t : t + 1, :])
        if c == chunks - 1:
            row = row + dot32(first_row(enter), gain, NT)
        maps[t, K:AUG, :] = row

    def step(i, _):
        s = top - 1 - i
        late = [maps[CHUNK * c + s + 1] for c in range(chunks)]
        gain = [g[CHUNK * c + s] for c in range(chunks)]
        out = [dot32(late[c], gain[c], NT) for c in range(chunks)]
        rows = [first_row(whole[pl.ds(CHUNK * c + s, 1), :]) for c in range(chunks)]
        for c in range(chunks):
            maps[CHUNK * c + s, 0:K, :] = out[c][:K]
            maps[CHUNK * c + s, K:AUG, :] = out[c][K:] + rows[c]
        pass_on(2 * i)
        pass_on(2 * i + 1)
        return 0

    lax.fori_loop(0, top, step, 0)
    for u in range(2 * top, units):
        pass_on(u)
    run = maps[CHUNK * (chunks - 1)]
    tails[chunks - 1] = run
    for c in range(chunks - 2, -1, -1):
        run = then(run, maps[CHUNK * c])
        tails[c] = run
    whole[...] = run
    for u in range(units):
        obs_out(u).wait()


def local_maps(last, at, gains, obs, means, transition):
    steps = gains.shape[0]
    chunks = steps // CHUNK
    rows, cols = obs.shape
    units = cols // (2 * WIDTH)
    return pl.pallas_call(
        lambda *refs: local_kernel(last, *refs),
        out_shape=(
            jax.ShapeDtypeStruct((steps, AUG, K), F32),
            jax.ShapeDtypeStruct((chunks, AUG, K), F32),
            jax.ShapeDtypeStruct((steps, K), F32),
            jax.ShapeDtypeStruct((AUG, K), F32),
            jax.ShapeDtypeStruct((units, rows, WIDTH), obs.dtype),
        ),
        in_specs=[SM, VM, HBM, VM],
        out_specs=(VM, VM, VM, VM, HBM),
        scratch_shapes=[
            pltpu.VMEM((units, rows, WIDTH), obs.dtype),
            pltpu.SemaphoreType.DMA((units,)),
            pltpu.SemaphoreType.DMA((units,)),
        ],
        compiler_params=params(44),
    )(at, gains, obs, jnp.concatenate([means, transition]))


def pick(refs, offset, count):
    offset = lax.rem(offset + count, count)
    out = refs[0][...]
    for i in range(1, count):
        out = jnp.where(offset == i, refs[i][...], out)
    return out


def four_kernel(dim, at, *refs):
    ins, (after, total) = refs[:SIDE], refs[SIDE:]
    mine = place(at[0])[dim]
    w = [pick(ins, other - mine, SIDE) for other in range(SIDE)]
    late, early = then(w[3], w[2]), then(w[1], w[0])
    total[...] = then(late, early)
    middle = then(late, w[1])
    tail = jnp.where(mine == 3, identity_map(), w[3])
    tail = jnp.where(mine == 1, late, tail)
    after[...] = jnp.where(mine == 0, middle, tail)


def pair_kernel(dim, at, mine, theirs, after, total):
    first = place(at[0])[dim] == 0
    late = jnp.where(first, theirs[...], mine[...])
    early = jnp.where(first, mine[...], theirs[...])
    after[...] = jnp.where(first, late, identity_map())
    total[...] = then(late, early)


def group_maps(kernel, dim, at, parts):
    one = jax.ShapeDtypeStruct((AUG, K), F32)
    return pl.pallas_call(
        lambda *refs: kernel(dim, *refs),
        out_shape=(one, one),
        in_specs=[SM] + [VM] * len(parts),
        out_specs=(VM, VM),
        compiler_params=params(4),
    )(at, *parts)


def apply_map(row, m):
    col = jnp.broadcast_to(row, (K, K)).T
    return jnp.sum(col * m[:K], axis=0, keepdims=True) + m[K : K + 1]


def final_kernel(at, *refs):
    ins = refs[:SIDE]
    by_x, by_core, by_z, tails, maps, shifted, smoothed, states = refs[SIDE:]
    steps = maps.shape[0]
    chunks = steps // CHUNK
    mine = place(at[0])[Y]
    v = jnp.zeros((1, K), F32)
    for other in range(SIDE - 1, 0, -1):
        v = jnp.where(other > mine, apply_map(v, pick(ins, other - mine, SIDE)), v)
    v = apply_map(v, by_x[...])
    v = apply_map(v, by_core[...])
    v = apply_map(v, by_z[...])
    col = jnp.broadcast_to(v, (K, K)).T
    for c in range(chunks):
        if c == chunks - 1:
            enter = col
        else:
            m = tails[c + 1]
            enter = jnp.sum(col * m[:K], axis=0, keepdims=True) + m[K : K + 1]
            enter = jnp.broadcast_to(enter, (K, K)).T
        rows = []
        for s in range(CHUNK):
            t = CHUNK * c + s
            rows.append(jnp.sum(enter * maps[t, 0:K, :], axis=0, keepdims=True) + maps[t, K : K + 1, :])
        out = jnp.concatenate(rows, axis=0) + shifted[CHUNK * c : CHUNK * (c + 1), :]
        smoothed[CHUNK * c : CHUNK * (c + 1), :] = out
    states[...] = smoothed[...].astype(BF16)


def final_states(at, parts, by_x, by_core, by_z, tails, maps, shifted):
    shape = shifted.shape
    return pl.pallas_call(
        final_kernel,
        out_shape=(jax.ShapeDtypeStruct(shape, F32), jax.ShapeDtypeStruct(shape, BF16)),
        in_specs=[SM] + [VM] * (SIDE + 6),
        out_specs=(VM, VM),
        compiler_params=params(4),
    )(at, *parts, by_x, by_core, by_z, tails, maps, shifted)


def routes(sizes, dim, hop_of):
    stride, total = 1, 1
    for s in sizes[dim + 1 :]:
        stride *= s
    for s in sizes:
        total *= s
    pairs = []
    for at in range(total):
        mine = (at // stride) % sizes[dim]
        pairs.append((at, at + ((mine + hop_of(at)) % sizes[dim] - mine) * stride))
    return pairs


def from_later(value, axis, sizes, dim):
    got = [value]
    for hop in range(1, sizes[dim]):
        got.append(lax.ppermute(value, axis, routes(sizes, dim, lambda _: -hop)))
    return got


LOW, HIGH = 0, 1
SPAN = 80.0
FOOT = 16


def put_coded(out, x):
    rows = x.shape[0]
    top = jnp.maximum(jnp.max(jnp.abs(x), axis=0, keepdims=True), 1e-30) * 1.0079
    top = top.astype(BF16).astype(F32)
    out[:rows, :] = jnp.exp(x * (SPAN / top)).astype(BF16)
    out[rows:, :] = jnp.broadcast_to(top, (FOOT, K)).astype(BF16)


def get_coded(coded):
    rows = coded.shape[0] - FOOT
    top = coded[rows:, :].astype(F32)[:1]
    return jnp.log(coded[:rows, :].astype(F32)) * (top * (1.0 / SPAN))


def stat_kernel(groups, adding, coded, scale, at, *refs):
    near, far, (obs_own, obs_far, load), refs = refs[:SIDE], refs[SIDE : 2 * SIDE], refs[2 * SIDE : 2 * SIDE + 3], refs[2 * SIDE + 3 :]
    adds, outs, (obs, rows_of, states, turned, sems) = refs[:adding], refs[adding:-5], refs[-5:]
    rows = near[0].shape[0]
    span = SIDE * rows
    y, x, core, z = place(at[0])

    def copies(i, j, offset, half):
        block = (y + jnp.where(core == 0, j, offset)) % SIDE * SIDE + (x + jnp.where(core == 0, offset, j)) % SIDE
        own = pl.multiple_of((2 * block + core) * WIDTH + half * HALF, HALF)
        return (
            pltpu.make_async_copy(obs_own.at[:, pl.ds(own, HALF)], obs.at[i, pl.ds(0, span)], sems.at[i, 0]),
            pltpu.make_async_copy(obs_far.at[block, :, pl.ds(half * HALF, HALF)], obs.at[i, pl.ds(span, span)], sems.at[i, 1]),
            pltpu.make_async_copy(load.at[pl.ds(own, HALF)], rows_of.at[i], sems.at[i, 2]),
        )

    jobs = [(n * SIDE + j, j, offset, half) for n, (offset, half) in enumerate(groups) for j in range(SIDE)]
    for job in jobs:
        for copy in copies(*job):
            copy.start()
    for hop in range(SIDE):
        top = pl.multiple_of((z + hop) % SIDE * rows, rows)
        states[pl.ds(top, rows), :] = near[hop][...]
        states[pl.ds(pl.multiple_of(top + span, rows), rows), :] = far[hop][...]
    turned[...] = states[...].T

    for first in range(0, len(jobs), 4):
        some = jobs[first : first + 4]
        for job in some:
            for copy in copies(*job):
                copy.wait()
        fits = [jnp.dot(rows_of[job[0]], turned[...], preferred_element_type=F32) for job in some]
        resids = [(f - obs[job[0]].T.astype(F32)).astype(BF16) for f, job in zip(fits, some)]
        terms = [jnp.dot(r, states[...], preferred_element_type=F32) * scale for r in resids]
        for (i, j, *_), term in zip(some, terms):
            if adding:
                term = term + get_coded(adds[i // SIDE].at[j])
            if coded:
                put_coded(outs[i // SIDE].at[j], term)
            else:
                outs[i // SIDE][j] = term


def stat_units(groups, adds, coded, scale, limit, at, near, far, obs_own, obs_far, load):
    n = SIDE * len(groups)
    rows = obs_own.shape[0]
    flops = n * HALF * rows * 2 * K * 4
    moved = n * HALF * (rows * 4 + K * 6)
    out = jax.ShapeDtypeStruct((SIDE, HALF + FOOT, K), BF16) if coded else jax.ShapeDtypeStruct((SIDE, HALF, K), F32)
    return pl.pallas_call(
        lambda *refs: stat_kernel(groups, len(adds), coded, scale, *refs),
        out_shape=[out] * len(groups),
        in_specs=[SM] + [VM] * (2 * SIDE) + [HBM] * 3 + [VM] * len(adds),
        out_specs=[VM] * len(groups),
        scratch_shapes=[
            pltpu.VMEM((n, 2 * rows, HALF), BF16),
            pltpu.VMEM((n, HALF, K), BF16),
            pltpu.VMEM((2 * rows, K), BF16),
            pltpu.VMEM((K, 2 * rows), BF16),
            pltpu.SemaphoreType.DMA((n, 3)),
        ],
        cost_estimate=pl.CostEstimate(flops=flops, bytes_accessed=moved, transcendentals=0),
        compiler_params=params(limit),
    )(at, *near, *far, obs_own, obs_far, load, *adds)


def join_kernel(*refs):
    ins, (two, one, three, own) = refs[:6], refs[6:]

    def total(d):
        halves = []
        for half in (LOW, HIGH):
            a, b, c = ins[3 * half : 3 * half + 3]
            halves.append(a[d] + get_coded(b.at[d]) + get_coded(c.at[d]))
        return jnp.concatenate(halves, axis=0)

    put_coded(two.at[0], total(2))
    put_coded(one.at[0], total(1))
    put_coded(three.at[0], total(3))
    own[...] = total(0)


def join_units(*parts):
    unit = jax.ShapeDtypeStruct((1, WIDTH + FOOT, K), BF16)
    return pl.pallas_call(
        join_kernel,
        out_shape=[unit, unit, unit, jax.ShapeDtypeStruct((WIDTH, K), F32)],
        in_specs=[VM] * 6,
        out_specs=[VM] * 4,
        compiler_params=params(12),
    )(*parts)


def last_kernel(own, two, one, three, out):
    out[...] = own[...] + get_coded(two.at[0]) + get_coded(one.at[0]) + get_coded(three.at[0])


def last_sum(own, *parts):
    return pl.pallas_call(
        last_kernel,
        out_shape=jax.ShapeDtypeStruct(own.shape, F32),
        in_specs=[VM] * 4,
        out_specs=VM,
        compiler_params=params(12),
    )(own, *parts)


def send(value, hop, first):
    pairs = [routes(TM, dim, lambda _: hop) for dim in (first, X + Y - first)]
    return lax.ppermute(value, "tm", [pairs[at % 2][at] for at in range(len(pairs[0]))])


def statistics(scale, at, near, far, obs_own, obs_far, load):
    args = (near, far, obs_own, obs_far, load)
    low, high = stat_units([(2, LOW), (2, HIGH)], (), True, scale, FAR_MIB, at, *args)
    got_low, got_high = send(low, 1, X), send(high, -1, X)
    at, low, high = lax.optimization_barrier((at, low, high))
    up_high, down_low = stat_units([(1, HIGH), (3, LOW)], (), True, scale, SIDE_MIB, at, *args)
    got_up_high, got_down_low = send(up_high, 1, X), send(down_low, -1, X)
    at, up_high, down_low = lax.optimization_barrier((at, up_high, down_low))
    up_low, down_high = stat_units([(1, LOW), (3, HIGH)], (got_low, got_high), True, scale, STEP_MIB, at, *args)
    got_up_low, got_down_high = send(up_low, 1, X), send(down_high, -1, X)
    at, up_low, down_high = lax.optimization_barrier((at, up_low, down_high))
    own_low, own_high = stat_units([(0, LOW), (0, HIGH)], (), False, scale, OWN_MIB, at, *args)
    two, one, three, own = join_units(own_low, got_up_low, got_down_low, own_high, got_up_high, got_down_high)
    return last_sum(own, send(two, 2, Y), send(one, 1, Y), send(three, -1, Y))


def body(gains, means, transition, observations, loadings):
    zones, times = lax.axis_size("zone"), lax.axis_size("tm")
    flip = routes(TM, CORE, lambda _: 1)
    swap = lambda value: lax.ppermute(value, "tm", flip)
    at = lax.axis_index(("tm", "zone")).astype(jnp.int32).reshape(1)
    maps, tails, shifted, whole, theirs = local_maps(times * zones - 1, at, gains, observations, means, transition)
    by_z, whole = group_maps(four_kernel, 3, at, from_later(whole, "zone", (zones,), 0))
    obs_far = swap(theirs)
    by_core, whole = group_maps(pair_kernel, CORE, at, from_later(whole, "tm", TM, CORE))
    by_x, whole = group_maps(four_kernel, X, at, from_later(whole, "tm", TM, X))
    whole, obs_far = lax.optimization_barrier((whole, obs_far))
    parts = from_later(whole, "tm", TM, Y)
    smoothed, states = final_states(at, parts, by_x, by_core, by_z, tails, maps, shifted)

    near = from_later(states, "zone", (zones,), 0)
    far = [swap(part) for part in near]
    total = times * zones * smoothed.shape[0]
    load_grad = statistics(1.0 / total, at, near, far, observations, obs_far, loadings)
    return (smoothed, load_grad)


def solution(mesh):
    return jax.shard_map(
        body,
        mesh=mesh,
        in_specs=(
            P(("tm", "zone"), None, None),
            P(("tm", "zone"), None),
            P(),
            P("tm", "zone"),
            P("zone", None),
        ),
        out_specs=(P(("tm", "zone"), None), P(("zone", "tm"), None)),
        check_vma=False,
    )
```

profile of v0, /device:TPU:6, one launch (start us, length us, event | category | flops | bytes accessed | tf_op | source)
XLA Modules:
  0.0 90.9 jit_solution(12388646240254919277)
XLA Ops:
  1.5 2.2 %copy-done.1 = f32[64,128,128]{2,1,0:T(8,128)S(1)} copy-done((f32[64,128,128]{2,1,0:T(8,128)S(1)}, f32[64,128,128]{2,1,0:T(8,128)}, u32[]{:S(2)}) %copy-start.1) | copy-done | bytes 4194328
  3.7 7.0 %shard_map.68 = (f32[64,136,128]{2,1,0:T(8,128)S(1)}, f32[8,136,128]{2,1,0:T(8,128)S(1)}, f32[64,128]{1,0:T(8,128)S(1)}, f32[136,128]{1,0:T(8,128)S(1)}, bf16[16,256,768]{2,1,0:T(8,128)(2,1)}) custom-call(s32[1]{0:T(128)} %bitcast.refs_0_.at, f32[64,128,128]{2,1,0:T(8,128)S(1)} %copy-done.1, bf16[256,24576]{1,0:T(8,128)(2,1)} %refs_9_.7, ...), custom_call_target="tpu_custom_call" | custom-call | tf_op jit(solution)/shard_map/pallas_call | solution.py:138
  10.7 2.0 %collective-permute-start.2 = (f32[136,128]{1,0:T(8,128)S(1)}, f32[136,128]{1,0:T(8,128)S(1)}, u32[]{:S(2)}, u32[]{:S(2)}) collective-permute-start(f32[136,128]{1,0:T(8,128)S(1)} %get-tuple-element.32.refs_1_), channel_id=1, source_target_pairs={{0,1},{1,2},{2,3},{3,0},{4,5},{5,6},{6,7},{7,4},{8,9},{9,10},{10,1... | collective-permute-start | bytes 208904 | tf_op jit(solution)/shard_map/ppermute | solution.py:258
  12.7 3.6 %collective-permute-start.1 = (f32[136,128]{1,0:T(8,128)S(1)}, f32[136,128]{1,0:T(8,128)S(1)}, u32[]{:S(2)}, u32[]{:S(2)}) collective-permute-start(f32[136,128]{1,0:T(8,128)S(1)} %get-tuple-element.32.refs_1_), channel_id=1, source_target_pairs={{0,2},{1,3},{2,0},{3,1},{4,6},{5,7},{6,4},{7,5},{8,10},{9,11},{10,... | collective-permute-start | bytes 208904 | tf_op jit(solution)/shard_map/ppermute | solution.py:258
  17.6 2.7 %collective-permute-done.1.refs_3_ = f32[136,128]{1,0:T(8,128)S(1)} collective-permute-done((f32[136,128]{1,0:T(8,128)S(1)}, f32[136,128]{1,0:T(8,128)S(1)}, u32[]{:S(2)}, u32[]{:S(2)}) %collective-permute-start.1) | collective-permute-done | bytes 69664 | tf_op jit(solution)/shard_map/ppermute | solution.py:258
  23.3 2.4 %collective-permute-start.5 = (f32[136,128]{1,0:T(8,128)S(1)}, f32[136,128]{1,0:T(8,128)S(1)}, u32[]{:S(2)}, u32[]{:S(2)}) collective-permute-start(f32[136,128]{1,0:T(8,128)S(1)} %get-tuple-element.34.refs_1_), channel_id=1, source_target_pairs={{0,16},{4,20},{8,24},{12,28},{16,0},{20,4},{24,8},{28,12},{32,48},... | collective-permute-start | bytes 208904 | tf_op jit(solution)/shard_map/ppermute | solution.py:258
  25.7 2.1 %collective-permute-done.6.refs_4_ = f32[136,128]{1,0:T(8,128)S(1)} collective-permute-done((f32[136,128]{1,0:T(8,128)S(1)}, f32[136,128]{1,0:T(8,128)S(1)}, u32[]{:S(2)}, u32[]{:S(2)}) %collective-permute-start.6) | collective-permute-done | bytes 69664 | tf_op jit(solution)/shard_map/ppermute | solution.py:258
  27.8 1.3 %collective-permute-done.5.refs_3_ = f32[136,128]{1,0:T(8,128)S(1)} collective-permute-done((f32[136,128]{1,0:T(8,128)S(1)}, f32[136,128]{1,0:T(8,128)S(1)}, u32[]{:S(2)}, u32[]{:S(2)}) %collective-permute-start.5) | collective-permute-done | bytes 69664 | tf_op jit(solution)/shard_map/ppermute | solution.py:258
  29.1 2.1 %collective-permute-done.4.refs_2_ = f32[136,128]{1,0:T(8,128)S(1)} collective-permute-done((f32[136,128]{1,0:T(8,128)S(1)}, f32[136,128]{1,0:T(8,128)S(1)}, u32[]{:S(2)}, u32[]{:S(2)}) %collective-permute-start.4) | collective-permute-done | bytes 69664 | tf_op jit(solution)/shard_map/ppermute | solution.py:258
  31.8 1.6 %collective-permute-start.10 = (f32[136,128]{1,0:T(8,128)S(1)}, f32[136,128]{1,0:T(8,128)S(1)}, u32[]{:S(2)}, u32[]{:S(2)}) collective-permute-start(f32[136,128]{1,0:T(8,128)S(1)} %get-tuple-element.37.refs_0_), channel_id=1, source_target_pairs={{0,32},{4,36},{8,40},{12,44},{16,48},{20,52},{24,56},{28,60},{32,6... | collective-permute-start | bytes 208904 | tf_op jit(solution)/shard_map/ppermute | solution.py:258
  33.5 2.9 %collective-permute-start.9 = (f32[136,128]{1,0:T(8,128)S(1)}, f32[136,128]{1,0:T(8,128)S(1)}, u32[]{:S(2)}, u32[]{:S(2)}) collective-permute-start(f32[136,128]{1,0:T(8,128)S(1)} %get-tuple-element.37.refs_0_), channel_id=1, source_target_pairs={{0,64},{4,68},{8,72},{12,76},{16,80},{20,84},{24,88},{28,92},{32,9... | collective-permute-start | bytes 208904 | tf_op jit(solution)/shard_map/ppermute | solution.py:258
  36.4 1.3 %collective-permute-start.8 = (f32[136,128]{1,0:T(8,128)S(1)}, f32[136,128]{1,0:T(8,128)S(1)}, u32[]{:S(2)}, u32[]{:S(2)}) collective-permute-start(f32[136,128]{1,0:T(8,128)S(1)} %get-tuple-element.37.refs_0_), channel_id=1, source_target_pairs={{0,96},{4,100},{8,104},{12,108},{16,112},{20,116},{24,120},{28,124... | collective-permute-start | bytes 208904 | tf_op jit(solution)/shard_map/ppermute | solution.py:258
  37.7 1.7 %collective-permute-done.9.refs_2_ = f32[136,128]{1,0:T(8,128)S(1)} collective-permute-done((f32[136,128]{1,0:T(8,128)S(1)}, f32[136,128]{1,0:T(8,128)S(1)}, u32[]{:S(2)}, u32[]{:S(2)}) %collective-permute-start.9) | collective-permute-done | bytes 69664 | tf_op jit(solution)/shard_map/ppermute | solution.py:258
  39.4 1.3 %collective-permute-done.8.refs_1_ = f32[136,128]{1,0:T(8,128)S(1)} collective-permute-done((f32[136,128]{1,0:T(8,128)S(1)}, f32[136,128]{1,0:T(8,128)S(1)}, u32[]{:S(2)}, u32[]{:S(2)}) %collective-permute-start.8) | collective-permute-done | bytes 69664 | tf_op jit(solution)/shard_map/ppermute | solution.py:258
  40.7 1.7 %shard_map.72 = (f32[64,128]{1,0:T(8,128)}, bf16[64,128]{1,0:T(8,128)(2,1)S(1)}) custom-call(s32[1]{0:T(128)} %bitcast.refs_0_.at, f32[136,128]{1,0:T(8,128)S(1)} %get-tuple-element.37.refs_0_, f32[136,128]{1,0:T(8,128)S(1)} %collective-permute-done.8.refs_1_, f32[136,128]{1,0:T(8,128)S(1)} %collective-permute-done.9.refs_2_, ...), custom_call_target="tpu_custom_call" | custom-call | tf_op jit(solution)/shard_map/pallas_call | solution.py:233
  43.2 3.2 %collective-permute-start.12 = (bf16[64,128]{1,0:T(8,128)(2,1)S(1)}, bf16[64,128]{1,0:T(8,128)(2,1)S(1)}, u32[]{:S(2)}, u32[]{:S(2)}) collective-permute-start(bf16[64,128]{1,0:T(8,128)(2,1)S(1)} %get-tuple-element.45.refs_1_), channel_id=1, source_target_pairs={{0,2},{1,3},{2,0},{3,1},{4,6},{5,7},{6,4},{7,5},{8,10},{9,11},{10,... | collective-permute-start | bytes 49160 | tf_op jit(solution)/shard_map/ppermute | solution.py:258
  48.4 1.6 %collective-permute-done.11.refs_2_ = bf16[64,128]{1,0:T(8,128)(2,1)S(1)} collective-permute-done((bf16[64,128]{1,0:T(8,128)(2,1)S(1)}, bf16[64,128]{1,0:T(8,128)(2,1)S(1)}, u32[]{:S(2)}, u32[]{:S(2)}) %collective-permute-start.11) | collective-permute-done | bytes 16416 | tf_op jit(solution)/shard_map/ppermute | solution.py:258
  51.3 4.0 %shard_map.73 = (bf16[4,400,128]{2,1,0:T(8,128)(2,1)S(1)}, bf16[4,400,128]{2,1,0:T(8,128)(2,1)S(1)}) custom-call(s32[1]{0:T(128)} %bitcast.refs_0_.at, bf16[64,128]{1,0:T(8,128)(2,1)S(1)} %get-tuple-element.45.refs_1_, bf16[64,128]{1,0:T(8,128)(2,1)S(1)} %collective-permute-done.11.refs_2_, bf16[64,128]{1,0:T(8,128)(2,1)S(1)} %collective-permute-done.12.refs_3_, ...), custom_call_target="tpu_custom_call" | custom-call | flops 805306368 | bytes 5505024 | tf_op jit(solution)/shard_map/pallas_call | solution.py:330
  55.9 1.4 %collective-permute-start.19 = (bf16[4,400,128]{2,1,0:T(8,128)(2,1)S(1)}, bf16[4,400,128]{2,1,0:T(8,128)(2,1)S(1)}, u32[]{:S(2)}, u32[]{:S(2)}) collective-permute-start(bf16[4,400,128]{2,1,0:T(8,128)(2,1)S(1)} %get-tuple-element.48), channel_id=1, source_target_pairs={{0,24},{4,100},{8,0},{12,108},{16,8},{20,116},{24,16},{28,124},{32... | collective-permute-start | bytes 1228808 | tf_op jit(solution)/shard_map/ppermute | solution.py:390
  57.4 4.0 %shard_map.74 = (bf16[4,400,128]{2,1,0:T(8,128)(2,1)S(1)}, bf16[4,400,128]{2,1,0:T(8,128)(2,1)S(1)}) custom-call(s32[1]{0:T(128)} %bitcast.refs_0_.at, bf16[64,128]{1,0:T(8,128)(2,1)S(1)} %get-tuple-element.45.refs_1_, bf16[64,128]{1,0:T(8,128)(2,1)S(1)} %collective-permute-done.11.refs_2_, bf16[64,128]{1,0:T(8,128)(2,1)S(1)} %collective-permute-done.12.refs_3_, ...), custom_call_target="tpu_custom_call" | custom-call | flops 805306368 | bytes 5505024 | tf_op jit(solution)/shard_map/pallas_call | solution.py:330
  61.4 1.9 %collective-permute-start.22 = (bf16[4,400,128]{2,1,0:T(8,128)(2,1)S(1)}, bf16[4,400,128]{2,1,0:T(8,128)(2,1)S(1)}, u32[]{:S(2)}, u32[]{:S(2)}) collective-permute-start(bf16[4,400,128]{2,1,0:T(8,128)(2,1)S(1)} %get-tuple-element.50), channel_id=1, source_target_pairs={{0,8},{4,36},{8,16},{12,44},{16,24},{20,52},{24,0},{28,60},{32,40}... | collective-permute-start | bytes 1228808 | tf_op jit(solution)/shard_map/ppermute | solution.py:390
  63.5 1.6 %collective-permute-done.19.refs_13_ = bf16[4,400,128]{2,1,0:T(8,128)(2,1)S(1)} collective-permute-done((bf16[4,400,128]{2,1,0:T(8,128)(2,1)S(1)}, bf16[4,400,128]{2,1,0:T(8,128)(2,1)S(1)}, u32[]{:S(2)}, u32[]{:S(2)}) %collective-permute-start.19) | collective-permute-done | bytes 409632 | tf_op jit(solution)/shard_map/ppermute | solution.py:390
  65.1 4.0 %shard_map.75 = (bf16[4,400,128]{2,1,0:T(8,128)(2,1)S(1)}, bf16[4,400,128]{2,1,0:T(8,128)(2,1)S(1)}) custom-call(s32[1]{0:T(128)} %bitcast.refs_0_.at, bf16[64,128]{1,0:T(8,128)(2,1)S(1)} %get-tuple-element.45.refs_1_, bf16[64,128]{1,0:T(8,128)(2,1)S(1)} %collective-permute-done.11.refs_2_, bf16[64,128]{1,0:T(8,128)(2,1)S(1)} %collective-permute-done.12.refs_3_, ...), custom_call_target="tpu_custom_call" | custom-call | flops 805306368 | bytes 5505024 | tf_op jit(solution)/shard_map/pallas_call | solution.py:330
  69.1 1.5 %collective-permute-start.20 = (bf16[4,400,128]{2,1,0:T(8,128)(2,1)S(1)}, bf16[4,400,128]{2,1,0:T(8,128)(2,1)S(1)}, u32[]{:S(2)}, u32[]{:S(2)}) collective-permute-start(bf16[4,400,128]{2,1,0:T(8,128)(2,1)S(1)} %get-tuple-element.53), channel_id=1, source_target_pairs={{0,8},{4,36},{8,16},{12,44},{16,24},{20,52},{24,0},{28,60},{32,40}... | collective-permute-start | bytes 1228808 | tf_op jit(solution)/shard_map/ppermute | solution.py:390
  71.2 3.5 %shard_map.76 = (f32[4,384,128]{2,1,0:T(8,128)S(1)}, f32[4,384,128]{2,1,0:T(8,128)S(1)}) custom-call(s32[1]{0:T(128)} %bitcast.refs_0_.at, bf16[64,128]{1,0:T(8,128)(2,1)S(1)} %get-tuple-element.45.refs_1_, bf16[64,128]{1,0:T(8,128)(2,1)S(1)} %collective-permute-done.11.refs_2_, bf16[64,128]{1,0:T(8,128)(2,1)S(1)} %collective-permute-done.12.refs_3_, ...), custom_call_target="tpu_custom_call" | custom-call | flops 805306368 | bytes 5505024 | tf_op jit(solution)/shard_map/pallas_call | solution.py:330
  74.8 2.4 %collective-permute-done.20.refs_1_ = bf16[4,400,128]{2,1,0:T(8,128)(2,1)S(1)} collective-permute-done((bf16[4,400,128]{2,1,0:T(8,128)(2,1)S(1)}, bf16[4,400,128]{2,1,0:T(8,128)(2,1)S(1)}, u32[]{:S(2)}, u32[]{:S(2)}) %collective-permute-start.20) | collective-permute-done | bytes 409632 | tf_op jit(solution)/shard_map/ppermute | solution.py:390
  77.1 2.6 %collective-permute-done.23.refs_5_ = bf16[4,400,128]{2,1,0:T(8,128)(2,1)S(1)} collective-permute-done((bf16[4,400,128]{2,1,0:T(8,128)(2,1)S(1)}, bf16[4,400,128]{2,1,0:T(8,128)(2,1)S(1)}, u32[]{:S(2)}, u32[]{:S(2)}) %collective-permute-start.23) | collective-permute-done | bytes 409632 | tf_op jit(solution)/shard_map/ppermute | solution.py:390
  80.5 1.6 %collective-permute-start.24 = (bf16[1,784,128]{2,1,0:T(8,128)(2,1)S(1)}, bf16[1,784,128]{2,1,0:T(8,128)(2,1)S(1)}, u32[]{:S(2)}, u32[]{:S(2)}) collective-permute-start(bf16[1,784,128]{2,1,0:T(8,128)(2,1)S(1)} %get-tuple-element.59), channel_id=1, source_target_pairs={{0,64},{4,20},{8,72},{12,28},{16,80},{20,4},{24,88},{28,12},{32,96... | collective-permute-start | bytes 602120 | tf_op jit(solution)/shard_map/ppermute | solution.py:390
  82.1 1.9 %collective-permute-start.25 = (bf16[1,784,128]{2,1,0:T(8,128)(2,1)S(1)}, bf16[1,784,128]{2,1,0:T(8,128)(2,1)S(1)}, u32[]{:S(2)}, u32[]{:S(2)}) collective-permute-start(bf16[1,784,128]{2,1,0:T(8,128)(2,1)S(1)} %get-tuple-element.60), channel_id=1, source_target_pairs={{0,32},{4,12},{8,40},{12,20},{16,48},{20,28},{24,56},{28,4},{32,64... | collective-permute-start | bytes 602120 | tf_op jit(solution)/shard_map/ppermute | solution.py:390
  84.0 1.4 %collective-permute-start.26 = (bf16[1,784,128]{2,1,0:T(8,128)(2,1)S(1)}, bf16[1,784,128]{2,1,0:T(8,128)(2,1)S(1)}, u32[]{:S(2)}, u32[]{:S(2)}) collective-permute-start(bf16[1,784,128]{2,1,0:T(8,128)(2,1)S(1)} %get-tuple-element.61), channel_id=1, source_target_pairs={{0,96},{4,28},{8,104},{12,4},{16,112},{20,12},{24,120},{28,20},{32... | collective-permute-start | bytes 602120 | tf_op jit(solution)/shard_map/ppermute | solution.py:390
  85.3 2.5 %collective-permute-done.24.two = bf16[1,784,128]{2,1,0:T(8,128)(2,1)S(1)} collective-permute-done((bf16[1,784,128]{2,1,0:T(8,128)(2,1)S(1)}, bf16[1,784,128]{2,1,0:T(8,128)(2,1)S(1)}, u32[]{:S(2)}, u32[]{:S(2)}) %collective-permute-start.24) | collective-permute-done | bytes 200736 | tf_op jit(solution)/shard_map/ppermute | solution.py:390
  87.9 2.1 %collective-permute-done.25.one = bf16[1,784,128]{2,1,0:T(8,128)(2,1)S(1)} collective-permute-done((bf16[1,784,128]{2,1,0:T(8,128)(2,1)S(1)}, bf16[1,784,128]{2,1,0:T(8,128)(2,1)S(1)}, u32[]{:S(2)}, u32[]{:S(2)}) %collective-permute-start.25) | collective-permute-done | bytes 200736 | tf_op jit(solution)/shard_map/ppermute | solution.py:390
  (43 shorter events, 13.1 us)
Async XLA Ops:
  1.5 2.2 %copy-start.1 = (f32[64,128,128]{2,1,0:T(8,128)S(1)}, f32[64,128,128]{2,1,0:T(8,128)}, u32[]{:S(2)}) copy-start(f32[64,128,128]{2,1,0:T(8,128)} %refs_1_.1) | copy-start | bytes 12582916
  10.7 21.1 %collective-permute-start.7 = (bf16[16,256,768]{2,1,0:T(8,128)(2,1)}, bf16[16,256,768]{2,1,0:T(8,128)(2,1)S(1)}, u32[]{:S(2)}, u32[]{:S(2)}) collective-permute-start(bf16[16,256,768]{2,1,0:T(8,128)(2,1)} %get-tuple-element.36), channel_id=1, source_target_pairs={{0,4},{4,0},{8,12},{12,8},{16,20},{20,16},{24,28},{28,24},{32,36},... | collective-permute-start | bytes 18874376 | tf_op jit(solution)/shard_map/ppermute | solution.py:412
  10.7 6.9 %collective-permute-start.2 = (f32[136,128]{1,0:T(8,128)S(1)}, f32[136,128]{1,0:T(8,128)S(1)}, u32[]{:S(2)}, u32[]{:S(2)}) collective-permute-start(f32[136,128]{1,0:T(8,128)S(1)} %get-tuple-element.32.refs_1_), channel_id=1, source_target_pairs={{0,1},{1,2},{2,3},{3,0},{4,5},{5,6},{6,7},{7,4},{8,9},{9,10},{10,1... | collective-permute-start | bytes 208904 | tf_op jit(solution)/shard_map/ppermute | solution.py:258
  12.7 7.6 %collective-permute-start.1 = (f32[136,128]{1,0:T(8,128)S(1)}, f32[136,128]{1,0:T(8,128)S(1)}, u32[]{:S(2)}, u32[]{:S(2)}) collective-permute-start(f32[136,128]{1,0:T(8,128)S(1)} %get-tuple-element.32.refs_1_), channel_id=1, source_target_pairs={{0,2},{1,3},{2,0},{3,1},{4,6},{5,7},{6,4},{7,5},{8,10},{9,11},{10,... | collective-permute-start | bytes 208904 | tf_op jit(solution)/shard_map/ppermute | solution.py:258
  16.3 4.3 %collective-permute-start = (f32[136,128]{1,0:T(8,128)S(1)}, f32[136,128]{1,0:T(8,128)S(1)}, u32[]{:S(2)}, u32[]{:S(2)}) collective-permute-start(f32[136,128]{1,0:T(8,128)S(1)} %get-tuple-element.32.refs_1_), channel_id=1, source_target_pairs={{0,3},{1,0},{2,1},{3,2},{4,7},{5,4},{6,5},{7,6},{8,11},{9,8},{10,9... | collective-permute-start | bytes 208904 | tf_op jit(solution)/shard_map/ppermute | solution.py:258
  21.2 1.3 %collective-permute-start.3 = (f32[136,128]{1,0:T(8,128)S(1)}, f32[136,128]{1,0:T(8,128)S(1)}, u32[]{:S(2)}, u32[]{:S(2)}) collective-permute-start(f32[136,128]{1,0:T(8,128)S(1)} %get-tuple-element.33.refs_1_), channel_id=1, source_target_pairs={{0,4},{4,0},{8,12},{12,8},{16,20},{20,16},{24,28},{28,24},{32,36},... | collective-permute-start | bytes 208904 | tf_op jit(solution)/shard_map/ppermute | solution.py:258
  22.7 5.1 %collective-permute-start.6 = (f32[136,128]{1,0:T(8,128)S(1)}, f32[136,128]{1,0:T(8,128)S(1)}, u32[]{:S(2)}, u32[]{:S(2)}) collective-permute-start(f32[136,128]{1,0:T(8,128)S(1)} %get-tuple-element.34.refs_1_), channel_id=1, source_target_pairs={{0,8},{4,12},{8,16},{12,20},{16,24},{20,28},{24,0},{28,4},{32,40},... | collective-permute-start | bytes 208904 | tf_op jit(solution)/shard_map/ppermute | solution.py:258
  23.3 5.8 %collective-permute-start.5 = (f32[136,128]{1,0:T(8,128)S(1)}, f32[136,128]{1,0:T(8,128)S(1)}, u32[]{:S(2)}, u32[]{:S(2)}) collective-permute-start(f32[136,128]{1,0:T(8,128)S(1)} %get-tuple-element.34.refs_1_), channel_id=1, source_target_pairs={{0,16},{4,20},{8,24},{12,28},{16,0},{20,4},{24,8},{28,12},{32,48},... | collective-permute-start | bytes 208904 | tf_op jit(solution)/shard_map/ppermute | solution.py:258
  25.7 5.5 %collective-permute-start.4 = (f32[136,128]{1,0:T(8,128)S(1)}, f32[136,128]{1,0:T(8,128)S(1)}, u32[]{:S(2)}, u32[]{:S(2)}) collective-permute-start(f32[136,128]{1,0:T(8,128)S(1)} %get-tuple-element.34.refs_1_), channel_id=1, source_target_pairs={{0,24},{4,28},{8,0},{12,4},{16,8},{20,12},{24,16},{28,20},{32,56},... | collective-permute-start | bytes 208904 | tf_op jit(solution)/shard_map/ppermute | solution.py:258
  31.8 19.5 %copy-start = (bf16[16,256,768]{2,1,0:T(8,128)(2,1)}, bf16[16,256,768]{2,1,0:T(8,128)(2,1)S(1)}, u32[]{:S(2)}) copy-start(bf16[16,256,768]{2,1,0:T(8,128)(2,1)S(1)} %collective-permute-done.7.refs_10_) | copy-start | bytes 18874372
  31.8 5.9 %collective-permute-start.10 = (f32[136,128]{1,0:T(8,128)S(1)}, f32[136,128]{1,0:T(8,128)S(1)}, u32[]{:S(2)}, u32[]{:S(2)}) collective-permute-start(f32[136,128]{1,0:T(8,128)S(1)} %get-tuple-element.37.refs_0_), channel_id=1, source_target_pairs={{0,32},{4,36},{8,40},{12,44},{16,48},{20,52},{24,56},{28,60},{32,6... | collective-permute-start | bytes 208904 | tf_op jit(solution)/shard_map/ppermute | solution.py:258
  33.5 5.9 %collective-permute-start.9 = (f32[136,128]{1,0:T(8,128)S(1)}, f32[136,128]{1,0:T(8,128)S(1)}, u32[]{:S(2)}, u32[]{:S(2)}) collective-permute-start(f32[136,128]{1,0:T(8,128)S(1)} %get-tuple-element.37.refs_0_), channel_id=1, source_target_pairs={{0,64},{4,68},{8,72},{12,76},{16,80},{20,84},{24,88},{28,92},{32,9... | collective-permute-start | bytes 208904 | tf_op jit(solution)/shard_map/ppermute | solution.py:258
  36.4 4.3 %collective-permute-start.8 = (f32[136,128]{1,0:T(8,128)S(1)}, f32[136,128]{1,0:T(8,128)S(1)}, u32[]{:S(2)}, u32[]{:S(2)}) collective-permute-start(f32[136,128]{1,0:T(8,128)S(1)} %get-tuple-element.37.refs_0_), channel_id=1, source_target_pairs={{0,96},{4,100},{8,104},{12,108},{16,112},{20,116},{24,120},{28,124... | collective-permute-start | bytes 208904 | tf_op jit(solution)/shard_map/ppermute | solution.py:258
  42.4 5.0 %collective-permute-start.13 = (bf16[64,128]{1,0:T(8,128)(2,1)S(1)}, bf16[64,128]{1,0:T(8,128)(2,1)S(1)}, u32[]{:S(2)}, u32[]{:S(2)}) collective-permute-start(bf16[64,128]{1,0:T(8,128)(2,1)S(1)} %get-tuple-element.45.refs_1_), channel_id=1, source_target_pairs={{0,1},{1,2},{2,3},{3,0},{4,5},{5,6},{6,7},{7,4},{8,9},{9,10},{10,1... | collective-permute-start | bytes 49160 | tf_op jit(solution)/shard_map/ppermute | solution.py:258
  43.2 5.2 %collective-permute-start.12 = (bf16[64,128]{1,0:T(8,128)(2,1)S(1)}, bf16[64,128]{1,0:T(8,128)(2,1)S(1)}, u32[]{:S(2)}, u32[]{:S(2)}) collective-permute-start(bf16[64,128]{1,0:T(8,128)(2,1)S(1)} %get-tuple-element.45.refs_1_), channel_id=1, source_target_pairs={{0,2},{1,3},{2,0},{3,1},{4,6},{5,7},{6,4},{7,5},{8,10},{9,11},{10,... | collective-permute-start | bytes 49160 | tf_op jit(solution)/shard_map/ppermute | solution.py:258
  46.4 3.7 %collective-permute-start.11 = (bf16[64,128]{1,0:T(8,128)(2,1)S(1)}, bf16[64,128]{1,0:T(8,128)(2,1)S(1)}, u32[]{:S(2)}, u32[]{:S(2)}) collective-permute-start(bf16[64,128]{1,0:T(8,128)(2,1)S(1)} %get-tuple-element.45.refs_1_), channel_id=1, source_target_pairs={{0,3},{1,0},{2,1},{3,2},{4,7},{5,4},{6,5},{7,6},{8,11},{9,8},{10,9... | collective-permute-start | bytes 49160 | tf_op jit(solution)/shard_map/ppermute | solution.py:258
  47.4 2.7 %collective-permute-start.14 = (bf16[64,128]{1,0:T(8,128)(2,1)S(1)}, bf16[64,128]{1,0:T(8,128)(2,1)S(1)}, u32[]{:S(2)}, u32[]{:S(2)}) collective-permute-start(bf16[64,128]{1,0:T(8,128)(2,1)S(1)} %get-tuple-element.45.refs_1_), channel_id=1, source_target_pairs={{0,4},{4,0},{8,12},{12,8},{16,20},{20,16},{24,28},{28,24},{32,36},... | collective-permute-start | bytes 49160 | tf_op jit(solution)/shard_map/ppermute | solution.py:412
  47.4 2.7 %collective-permute-start.17 = (bf16[64,128]{1,0:T(8,128)(2,1)S(1)}, bf16[64,128]{1,0:T(8,128)(2,1)S(1)}, u32[]{:S(2)}, u32[]{:S(2)}) collective-permute-start(bf16[64,128]{1,0:T(8,128)(2,1)S(1)} %collective-permute-done.13.refs_4_), channel_id=1, source_target_pairs={{0,4},{4,0},{8,12},{12,8},{16,20},{20,16},{24,28},{28,24},{32,36},... | collective-permute-start | bytes 49160 | tf_op jit(solution)/shard_map/ppermute | solution.py:412
  48.4 1.7 %collective-permute-start.16 = (bf16[64,128]{1,0:T(8,128)(2,1)S(1)}, bf16[64,128]{1,0:T(8,128)(2,1)S(1)}, u32[]{:S(2)}, u32[]{:S(2)}) collective-permute-start(bf16[64,128]{1,0:T(8,128)(2,1)S(1)} %collective-permute-done.12.refs_3_), channel_id=1, source_target_pairs={{0,4},{4,0},{8,12},{12,8},{16,20},{20,16},{24,28},{28,24},{32,36},... | collective-permute-start | bytes 49160 | tf_op jit(solution)/shard_map/ppermute | solution.py:412
  50.1 1.2 %collective-permute-start.15 = (bf16[64,128]{1,0:T(8,128)(2,1)S(1)}, bf16[64,128]{1,0:T(8,128)(2,1)S(1)}, u32[]{:S(2)}, u32[]{:S(2)}) collective-permute-start(bf16[64,128]{1,0:T(8,128)(2,1)S(1)} %collective-permute-done.11.refs_2_), channel_id=1, source_target_pairs={{0,4},{4,0},{8,12},{12,8},{16,20},{20,16},{24,28},{28,24},{32,36},... | collective-permute-start | bytes 49160 | tf_op jit(solution)/shard_map/ppermute | solution.py:412
  55.3 8.2 %collective-permute-start.18 = (bf16[4,400,128]{2,1,0:T(8,128)(2,1)S(1)}, bf16[4,400,128]{2,1,0:T(8,128)(2,1)S(1)}, u32[]{:S(2)}, u32[]{:S(2)}) collective-permute-start(bf16[4,400,128]{2,1,0:T(8,128)(2,1)S(1)} %get-tuple-element.47), channel_id=1, source_target_pairs={{0,8},{4,36},{8,16},{12,44},{16,24},{20,52},{24,0},{28,60},{32,40}... | collective-permute-start | bytes 1228808 | tf_op jit(solution)/shard_map/ppermute | solution.py:390
  55.9 9.2 %collective-permute-start.19 = (bf16[4,400,128]{2,1,0:T(8,128)(2,1)S(1)}, bf16[4,400,128]{2,1,0:T(8,128)(2,1)S(1)}, u32[]{:S(2)}, u32[]{:S(2)}) collective-permute-start(bf16[4,400,128]{2,1,0:T(8,128)(2,1)S(1)} %get-tuple-element.48), channel_id=1, source_target_pairs={{0,24},{4,100},{8,0},{12,108},{16,8},{20,116},{24,16},{28,124},{32... | collective-permute-start | bytes 1228808 | tf_op jit(solution)/shard_map/ppermute | solution.py:390
  61.4 13.4 %collective-permute-start.22 = (bf16[4,400,128]{2,1,0:T(8,128)(2,1)S(1)}, bf16[4,400,128]{2,1,0:T(8,128)(2,1)S(1)}, u32[]{:S(2)}, u32[]{:S(2)}) collective-permute-start(bf16[4,400,128]{2,1,0:T(8,128)(2,1)S(1)} %get-tuple-element.50), channel_id=1, source_target_pairs={{0,8},{4,36},{8,16},{12,44},{16,24},{20,52},{24,0},{28,60},{32,40}... | collective-permute-start | bytes 1228808 | tf_op jit(solution)/shard_map/ppermute | solution.py:390
  63.2 7.9 %slice-start = ((s8[6291456]{0:T(1024)(128)(4,1)}), s8[4194304]{0:T(1024)(128)(4,1)S(1)}, s32[]{:S(2)}) async-start(s8[6291456]{0:T(1024)(128)(4,1)} %bitcast.1), calls=%async_computation | async-start | bytes 8388608
  63.3 7.9 %slice-start.1 = ((s8[6291456]{0:T(1024)(128)(4,1)}), s8[2097152]{0:T(1024)(128)(4,1)S(1)}, s32[]{:S(2)}) async-start(s8[6291456]{0:T(1024)(128)(4,1)} %bitcast.1), calls=%async_computation.1 | async-start | bytes 4194304
  63.3 11.5 %collective-permute-start.21 = (bf16[4,400,128]{2,1,0:T(8,128)(2,1)S(1)}, bf16[4,400,128]{2,1,0:T(8,128)(2,1)S(1)}, u32[]{:S(2)}, u32[]{:S(2)}) collective-permute-start(bf16[4,400,128]{2,1,0:T(8,128)(2,1)S(1)} %get-tuple-element.51), channel_id=1, source_target_pairs={{0,24},{4,100},{8,0},{12,108},{16,8},{20,116},{24,16},{28,124},{32... | collective-permute-start | bytes 1228808 | tf_op jit(solution)/shard_map/ppermute | solution.py:390
  69.1 8.0 %collective-permute-start.20 = (bf16[4,400,128]{2,1,0:T(8,128)(2,1)S(1)}, bf16[4,400,128]{2,1,0:T(8,128)(2,1)S(1)}, u32[]{:S(2)}, u32[]{:S(2)}) collective-permute-start(bf16[4,400,128]{2,1,0:T(8,128)(2,1)S(1)} %get-tuple-element.53), channel_id=1, source_target_pairs={{0,8},{4,36},{8,16},{12,44},{16,24},{20,52},{24,0},{28,60},{32,40}... | collective-permute-start | bytes 1228808 | tf_op jit(solution)/shard_map/ppermute | solution.py:390
  70.6 9.2 %collective-permute-start.23 = (bf16[4,400,128]{2,1,0:T(8,128)(2,1)S(1)}, bf16[4,400,128]{2,1,0:T(8,128)(2,1)S(1)}, u32[]{:S(2)}, u32[]{:S(2)}) collective-permute-start(bf16[4,400,128]{2,1,0:T(8,128)(2,1)S(1)} %get-tuple-element.54), channel_id=1, source_target_pairs={{0,24},{4,100},{8,0},{12,108},{16,8},{20,116},{24,16},{28,124},{32... | collective-permute-start | bytes 1228808 | tf_op jit(solution)/shard_map/ppermute | solution.py:390
  80.5 7.4 %collective-permute-start.24 = (bf16[1,784,128]{2,1,0:T(8,128)(2,1)S(1)}, bf16[1,784,128]{2,1,0:T(8,128)(2,1)S(1)}, u32[]{:S(2)}, u32[]{:S(2)}) collective-permute-start(bf16[1,784,128]{2,1,0:T(8,128)(2,1)S(1)} %get-tuple-element.59), channel_id=1, source_target_pairs={{0,64},{4,20},{8,72},{12,28},{16,80},{20,4},{24,88},{28,12},{32,96... | collective-permute-start | bytes 602120 | tf_op jit(solution)/shard_map/ppermute | solution.py:390
  82.1 7.8 %collective-permute-start.25 = (bf16[1,784,128]{2,1,0:T(8,128)(2,1)S(1)}, bf16[1,784,128]{2,1,0:T(8,128)(2,1)S(1)}, u32[]{:S(2)}, u32[]{:S(2)}) collective-permute-start(bf16[1,784,128]{2,1,0:T(8,128)(2,1)S(1)} %get-tuple-element.60), channel_id=1, source_target_pairs={{0,32},{4,12},{8,40},{12,20},{16,48},{20,28},{24,56},{28,4},{32,64... | collective-permute-start | bytes 602120 | tf_op jit(solution)/shard_map/ppermute | solution.py:390
  84.0 6.0 %collective-permute-start.26 = (bf16[1,784,128]{2,1,0:T(8,128)(2,1)S(1)}, bf16[1,784,128]{2,1,0:T(8,128)(2,1)S(1)}, u32[]{:S(2)}, u32[]{:S(2)}) collective-permute-start(bf16[1,784,128]{2,1,0:T(8,128)(2,1)S(1)} %get-tuple-element.61), channel_id=1, source_target_pairs={{0,96},{4,28},{8,104},{12,4},{16,112},{20,12},{24,120},{28,20},{32... | collective-permute-start | bytes 602120 | tf_op jit(solution)/shard_map/ppermute | solution.py:390
where the time goes:
time: 91.1 us; the launch traced here: 90.9 us
  starting transfers between devices  32.2 us (35%)
  waiting for transfers between devices  27.6 us (30%)
  Pallas kernels  27.2 us (30%)
  local copies, waits for them, and re-layouts  2.19 us (2%)
    ppermute x13, starting transfers between devices, from_later(): got.append(lax.ppermute(value, axis, routes(sizes, dim, lambda _: -hop)))  20.5 us
    pallas_call x4, Pallas kernels, stat_units(): pl.pallas_call(lambda *refs: stat_kernel(groups, len(adds), coded, scale,...  15.5 us
    ppermute x13, waiting for transfers between devices, from_later(): got.append(lax.ppermute(value, axis, routes(sizes, dim, lambda _: -hop)))  15.2 us
    ppermute x9, waiting for transfers between devices, send(): lax.ppermute(value, 'tm', [pairs[at % 2][at] for at in range(len(pairs[0]...  11.2 us
    ppermute x9, starting transfers between devices, send(): lax.ppermute(value, 'tm', [pairs[at % 2][at] for at in range(len(pairs[0]...  11.1 us
    pallas_call x1, Pallas kernels, local_maps(): pl.pallas_call(lambda *refs: local_kernel(last, *refs), out_shape=(jax.Sh...  6.97 us
    unnamed x8, local copies, waits for them, and re-layouts  2.19 us
  transfers between devices with their start and end apart: 27, of which 17 were waited for; matrix products, arithmetic and copies ran while one was open for 0% of the time, Pallas kernels for 14%

commit v1 on v0

--- a/solution.py
+++ b/solution.py
@@ -120,12 +120,20 @@
     lax.fori_loop(0, top, step, 0)
     for u in range(2 * top, units):
         pass_on(u)
-    run = maps[CHUNK * (chunks - 1)]
-    tails[chunks - 1] = run
-    for c in range(chunks - 2, -1, -1):
-        run = then(run, maps[CHUNK * c])
-        tails[c] = run
-    whole[...] = run
+    runs = {(c, c): maps[CHUNK * c] for c in range(chunks)}
+    size = 1
+    while size < chunks:
+        for c in range(0, chunks, 2 * size):
+            runs[c + 2 * size - 1, c] = then(runs[c + 2 * size - 1, c + size], runs[c + size - 1, c])
+        size *= 2
+    top = chunks - 1
+    while size > 1:
+        size //= 2
+        for c in range(size, chunks - size, 2 * size):
+            runs[top, c] = then(runs[top, c + size], runs[c + size - 1, c])
+    for c in range(chunks):
+        tails[c] = runs[top, c]
+    whole[...] = runs[top, 0]
     for u in range(units):
         obs_out(u).wait()
 
@@ -278,11 +286,12 @@
     return jnp.log(coded[:rows, :].astype(F32)) * (top * (1.0 / SPAN))
 
 
-def stat_kernel(groups, adding, coded, scale, at, *refs):
-    near, far, (obs_own, obs_far, load), refs = refs[:SIDE], refs[SIDE : 2 * SIDE], refs[2 * SIDE : 2 * SIDE + 3], refs[2 * SIDE + 3 :]
-    adds, outs, (obs, rows_of, states, turned, sems) = refs[:adding], refs[adding:-5], refs[-5:]
-    rows = near[0].shape[0]
-    span = SIDE * rows
+def stat_kernel(groups, known, adding, coded, scale, at, *refs):
+    fresh, sides, (obs_own, obs_far, load), refs = known == 2 * SIDE, refs[:known], refs[known : known + 3], refs[known + 3 :]
+    adds, outs, (obs, rows_of, sems) = refs[:adding], refs[adding:-3], refs[-3:]
+    states, turned = outs[-2:] if fresh else sides
+    span = obs_own.shape[0]
+    rows = span // SIDE
     y, x, core, z = place(at[0])
 
     def copies(i, j, offset, half):
@@ -298,11 +307,12 @@
     for job in jobs:
         for copy in copies(*job):
             copy.start()
-    for hop in range(SIDE):
-        top = pl.multiple_of((z + hop) % SIDE * rows, rows)
-        states[pl.ds(top, rows), :] = near[hop][...]
-        states[pl.ds(pl.multiple_of(top + span, rows), rows), :] = far[hop][...]
-    turned[...] = states[...].T
+    if fresh:
+        for hop in range(SIDE):
+            top = pl.multiple_of((z + hop) % SIDE * rows, rows)
+            states[pl.ds(top, rows), :] = sides[hop][...]
+            states[pl.ds(pl.multiple_of(top + span, rows), rows), :] = sides[SIDE + hop][...]
+        turned[...] = states[...].T
 
     for first in range(0, len(jobs), 4):
         some = jobs[first : first + 4]
@@ -321,27 +331,26 @@
                 outs[i // SIDE][j] = term
 
 
-def stat_units(groups, adds, coded, scale, limit, at, near, far, obs_own, obs_far, load):
+def stat_units(groups, adds, coded, scale, limit, at, sides, obs_own, obs_far, load):
     n = SIDE * len(groups)
     rows = obs_own.shape[0]
     flops = n * HALF * rows * 2 * K * 4
     moved = n * HALF * (rows * 4 + K * 6)
+    made = [jax.ShapeDtypeStruct(shape, BF16) for shape in ((2 * rows, K), (K, 2 * rows)) if len(sides) > 2]
     out = jax.ShapeDtypeStruct((SIDE, HALF + FOOT, K), BF16) if coded else jax.ShapeDtypeStruct((SIDE, HALF, K), F32)
     return pl.pallas_call(
-        lambda *refs: stat_kernel(groups, len(adds), coded, scale, *refs),
-        out_shape=[out] * len(groups),
-        in_specs=[SM] + [VM] * (2 * SIDE) + [HBM] * 3 + [VM] * len(adds),
-        out_specs=[VM] * len(groups),
+        lambda *refs: stat_kernel(groups, len(sides), len(adds), coded, scale, *refs),
+        out_shape=[out] * len(groups) + made,
+        in_specs=[SM] + [VM] * len(sides) + [HBM] * 3 + [VM] * len(adds),
+        out_specs=[VM] * (len(groups) + len(made)),
         scratch_shapes=[
             pltpu.VMEM((n, 2 * rows, HALF), BF16),
             pltpu.VMEM((n, HALF, K), BF16),
-            pltpu.VMEM((2 * rows, K), BF16),
-            pltpu.VMEM((K, 2 * rows), BF16),
             pltpu.SemaphoreType.DMA((n, 3)),
         ],
         cost_estimate=pl.CostEstimate(flops=flops, bytes_accessed=moved, transcendentals=0),
         compiler_params=params(limit),
-    )(at, *near, *far, obs_own, obs_far, load, *adds)
+    )(at, *sides, obs_own, obs_far, load, *adds)
 
 
 def join_kernel(*refs):
@@ -391,8 +400,9 @@
 
 
 def statistics(scale, at, near, far, obs_own, obs_far, load):
-    args = (near, far, obs_own, obs_far, load)
-    low, high = stat_units([(2, LOW), (2, HIGH)], (), True, scale, FAR_MIB, at, *args)
+    load = (obs_own, obs_far, load)
+    low, high, *sides = stat_units([(2, LOW), (2, HIGH)], (), True, scale, FAR_MIB, at, near + far, *load)
+    args = (sides, *load)
     got_low, got_high = send(low, 1, X), send(high, -1, X)
     at, low, high = lax.optimization_barrier((at, low, high))
     up_high, down_low = stat_units([(1, HIGH), (3, LOW)], (), True, scale, SIDE_MIB, at, *args)

time: 91.1 us -> 91.1 us (level)
  no operation moved by 1% of the time
where the time goes in v1:
time: 91.1 us; the launch traced here: 90.9 us
  starting transfers between devices  32.4 us (36%)
  waiting for transfers between devices  27.6 us (30%)
  Pallas kernels  27 us (30%)
  local copies, waits for them, and re-layouts  2.19 us (2%)
    ppermute x13, starting transfers between devices, from_later(): got.append(lax.ppermute(value, axis, routes(sizes, dim, lambda _: -hop)))  20.5 us
    pallas_call x4, Pallas kernels, stat_units(): pl.pallas_call(lambda *refs: stat_kernel(groups, len(sides), len(adds), c...  15.4 us
    ppermute x13, waiting for transfers between devices, from_later(): got.append(lax.ppermute(value, axis, routes(sizes, dim, lambda _: -hop)))  15.2 us
    ppermute x9, starting transfers between devices, send(): lax.ppermute(value, 'tm', [pairs[at % 2][at] for at in range(len(pairs[0]...  11.3 us
    ppermute x9, waiting for transfers between devices, send(): lax.ppermute(value, 'tm', [pairs[at % 2][at] for at in range(len(pairs[0]...  11.2 us
    pallas_call x1, Pallas kernels, local_maps(): pl.pallas_call(lambda *refs: local_kernel(last, *refs), out_shape=(jax.Sh...  6.87 us
    unnamed x8, local copies, waits for them, and re-layouts  2.19 us
  transfers between devices with their start and end apart: 27, of which 17 were waited for; matrix products, arithmetic and copies ran while one was open for 0% of the time, Pallas kernels for 14%

profile of v1, /device:TPU:6, one launch (start us, length us, event | category | flops | bytes accessed | tf_op | source)
XLA Modules:
  0.0 90.9 jit_solution(14918780060020848633)
XLA Ops:
  1.5 2.2 %copy-done.1 = f32[64,128,128]{2,1,0:T(8,128)S(1)} copy-done((f32[64,128,128]{2,1,0:T(8,128)S(1)}, f32[64,128,128]{2,1,0:T(8,128)}, u32[]{:S(2)}) %copy-start.1) | copy-done | bytes 4194328
  3.7 6.9 %shard_map.68 = (f32[64,136,128]{2,1,0:T(8,128)S(1)}, f32[8,136,128]{2,1,0:T(8,128)S(1)}, f32[64,128]{1,0:T(8,128)S(1)}, f32[136,128]{1,0:T(8,128)S(1)}, bf16[16,256,768]{2,1,0:T(8,128)(2,1)}) custom-call(s32[1]{0:T(128)} %bitcast.refs_0_.at, f32[64,128,128]{2,1,0:T(8,128)S(1)} %copy-done.1, bf16[256,24576]{1,0:T(8,128)(2,1)} %refs_3_.5, ...), custom_call_target="tpu_custom_call" | custom-call | tf_op jit(solution)/shard_map/pallas_call | solution.py:146
  10.6 2.0 %collective-permute-start.2 = (f32[136,128]{1,0:T(8,128)S(1)}, f32[136,128]{1,0:T(8,128)S(1)}, u32[]{:S(2)}, u32[]{:S(2)}) collective-permute-start(f32[136,128]{1,0:T(8,128)S(1)} %get-tuple-element.34.refs_1_), channel_id=1, source_target_pairs={{0,1},{1,2},{2,3},{3,0},{4,5},{5,6},{6,7},{7,4},{8,9},{9,10},{10,1... | collective-permute-start | bytes 208904 | tf_op jit(solution)/shard_map/ppermute | solution.py:266
  12.6 3.6 %collective-permute-start.1 = (f32[136,128]{1,0:T(8,128)S(1)}, f32[136,128]{1,0:T(8,128)S(1)}, u32[]{:S(2)}, u32[]{:S(2)}) collective-permute-start(f32[136,128]{1,0:T(8,128)S(1)} %get-tuple-element.34.refs_1_), channel_id=1, source_target_pairs={{0,2},{1,3},{2,0},{3,1},{4,6},{5,7},{6,4},{7,5},{8,10},{9,11},{10,... | collective-permute-start | bytes 208904 | tf_op jit(solution)/shard_map/ppermute | solution.py:266
  17.5 2.7 %collective-permute-done.1.refs_3_ = f32[136,128]{1,0:T(8,128)S(1)} collective-permute-done((f32[136,128]{1,0:T(8,128)S(1)}, f32[136,128]{1,0:T(8,128)S(1)}, u32[]{:S(2)}, u32[]{:S(2)}) %collective-permute-start.1) | collective-permute-done | bytes 69664 | tf_op jit(solution)/shard_map/ppermute | solution.py:266
  23.2 2.4 %collective-permute-start.5 = (f32[136,128]{1,0:T(8,128)S(1)}, f32[136,128]{1,0:T(8,128)S(1)}, u32[]{:S(2)}, u32[]{:S(2)}) collective-permute-start(f32[136,128]{1,0:T(8,128)S(1)} %get-tuple-element.36.refs_1_), channel_id=1, source_target_pairs={{0,16},{4,20},{8,24},{12,28},{16,0},{20,4},{24,8},{28,12},{32,48},... | collective-permute-start | bytes 208904 | tf_op jit(solution)/shard_map/ppermute | solution.py:266
  25.6 2.1 %collective-permute-done.6.refs_4_ = f32[136,128]{1,0:T(8,128)S(1)} collective-permute-done((f32[136,128]{1,0:T(8,128)S(1)}, f32[136,128]{1,0:T(8,128)S(1)}, u32[]{:S(2)}, u32[]{:S(2)}) %collective-permute-start.6) | collective-permute-done | bytes 69664 | tf_op jit(solution)/shard_map/ppermute | solution.py:266
  27.7 1.3 %collective-permute-done.5.refs_3_ = f32[136,128]{1,0:T(8,128)S(1)} collective-permute-done((f32[136,128]{1,0:T(8,128)S(1)}, f32[136,128]{1,0:T(8,128)S(1)}, u32[]{:S(2)}, u32[]{:S(2)}) %collective-permute-start.5) | collective-permute-done | bytes 69664 | tf_op jit(solution)/shard_map/ppermute | solution.py:266
  29.0 2.1 %collective-permute-done.4.refs_2_ = f32[136,128]{1,0:T(8,128)S(1)} collective-permute-done((f32[136,128]{1,0:T(8,128)S(1)}, f32[136,128]{1,0:T(8,128)S(1)}, u32[]{:S(2)}, u32[]{:S(2)}) %collective-permute-start.4) | collective-permute-done | bytes 69664 | tf_op jit(solution)/shard_map/ppermute | solution.py:266
  31.7 1.6 %collective-permute-start.10 = (f32[136,128]{1,0:T(8,128)S(1)}, f32[136,128]{1,0:T(8,128)S(1)}, u32[]{:S(2)}, u32[]{:S(2)}) collective-permute-start(f32[136,128]{1,0:T(8,128)S(1)} %get-tuple-element.39.refs_0_), channel_id=1, source_target_pairs={{0,32},{4,36},{8,40},{12,44},{16,48},{20,52},{24,56},{28,60},{32,6... | collective-permute-start | bytes 208904 | tf_op jit(solution)/shard_map/ppermute | solution.py:266
  33.3 2.9 %collective-permute-start.9 = (f32[136,128]{1,0:T(8,128)S(1)}, f32[136,128]{1,0:T(8,128)S(1)}, u32[]{:S(2)}, u32[]{:S(2)}) collective-permute-start(f32[136,128]{1,0:T(8,128)S(1)} %get-tuple-element.39.refs_0_), channel_id=1, source_target_pairs={{0,64},{4,68},{8,72},{12,76},{16,80},{20,84},{24,88},{28,92},{32,9... | collective-permute-start | bytes 208904 | tf_op jit(solution)/shard_map/ppermute | solution.py:266
  36.2 1.3 %collective-permute-start.8 = (f32[136,128]{1,0:T(8,128)S(1)}, f32[136,128]{1,0:T(8,128)S(1)}, u32[]{:S(2)}, u32[]{:S(2)}) collective-permute-start(f32[136,128]{1,0:T(8,128)S(1)} %get-tuple-element.39.refs_0_), channel_id=1, source_target_pairs={{0,96},{4,100},{8,104},{12,108},{16,112},{20,116},{24,120},{28,124... | collective-permute-start | bytes 208904 | tf_op jit(solution)/shard_map/ppermute | solution.py:266
  37.6 1.7 %collective-permute-done.9.refs_2_ = f32[136,128]{1,0:T(8,128)S(1)} collective-permute-done((f32[136,128]{1,0:T(8,128)S(1)}, f32[136,128]{1,0:T(8,128)S(1)}, u32[]{:S(2)}, u32[]{:S(2)}) %collective-permute-start.9) | collective-permute-done | bytes 69664 | tf_op jit(solution)/shard_map/ppermute | solution.py:266
  39.3 1.3 %collective-permute-done.8.refs_1_ = f32[136,128]{1,0:T(8,128)S(1)} collective-permute-done((f32[136,128]{1,0:T(8,128)S(1)}, f32[136,128]{1,0:T(8,128)S(1)}, u32[]{:S(2)}, u32[]{:S(2)}) %collective-permute-start.8) | collective-permute-done | bytes 69664 | tf_op jit(solution)/shard_map/ppermute | solution.py:266
  40.6 1.7 %shard_map.72 = (f32[64,128]{1,0:T(8,128)}, bf16[64,128]{1,0:T(8,128)(2,1)S(1)}) custom-call(s32[1]{0:T(128)} %bitcast.refs_0_.at, f32[136,128]{1,0:T(8,128)S(1)} %get-tuple-element.39.refs_0_, f32[136,128]{1,0:T(8,128)S(1)} %collective-permute-done.8.refs_1_, f32[136,128]{1,0:T(8,128)S(1)} %collective-permute-done.9.refs_2_, ...), custom_call_target="tpu_custom_call" | custom-call | tf_op jit(solution)/shard_map/pallas_call | solution.py:241
  43.1 3.2 %collective-permute-start.12 = (bf16[64,128]{1,0:T(8,128)(2,1)S(1)}, bf16[64,128]{1,0:T(8,128)(2,1)S(1)}, u32[]{:S(2)}, u32[]{:S(2)}) collective-permute-start(bf16[64,128]{1,0:T(8,128)(2,1)S(1)} %get-tuple-element.47.refs_1_), channel_id=1, source_target_pairs={{0,2},{1,3},{2,0},{3,1},{4,6},{5,7},{6,4},{7,5},{8,10},{9,11},{10,... | collective-permute-start | bytes 49160 | tf_op jit(solution)/shard_map/ppermute | solution.py:266
  48.3 1.7 %collective-permute-done.11.refs_2_ = bf16[64,128]{1,0:T(8,128)(2,1)S(1)} collective-permute-done((bf16[64,128]{1,0:T(8,128)(2,1)S(1)}, bf16[64,128]{1,0:T(8,128)(2,1)S(1)}, u32[]{:S(2)}, u32[]{:S(2)}) %collective-permute-start.11) | collective-permute-done | bytes 16416 | tf_op jit(solution)/shard_map/ppermute | solution.py:266
  51.2 4.0 %shard_map.73 = (bf16[4,400,128]{2,1,0:T(8,128)(2,1)S(1)}, bf16[4,400,128]{2,1,0:T(8,128)(2,1)S(1)}, bf16[512,128]{1,0:T(8,128)(2,1)S(1)}, bf16[128,512]{1,0:T(8,128)(2,1)S(1)}) custom-call(s32[1]{0:T(128)} %bitcast.refs_0_.at, bf16[64,128]{1,0:T(8,128)(2,1)S(1)} %get-tuple-element.47.refs_1_, bf16[64,128]{1,0:T(8,128)(2,1)S(1)} %collective-permute-done.11.refs_2_, ...), custom_call_target="tpu_custom_call" | custom-call | flops 805306368 | bytes 5505024 | tf_op jit(solution)/shard_map/pallas_call | solution.py:341
  56.0 1.4 %collective-permute-start.19 = (bf16[4,400,128]{2,1,0:T(8,128)(2,1)S(1)}, bf16[4,400,128]{2,1,0:T(8,128)(2,1)S(1)}, u32[]{:S(2)}, u32[]{:S(2)}) collective-permute-start(bf16[4,400,128]{2,1,0:T(8,128)(2,1)S(1)} %get-tuple-element.50), channel_id=1, source_target_pairs={{0,24},{4,100},{8,0},{12,108},{16,8},{20,116},{24,16},{28,124},{32... | collective-permute-start | bytes 1228808 | tf_op jit(solution)/shard_map/ppermute | solution.py:399
  57.5 4.0 %shard_map.74 = (bf16[4,400,128]{2,1,0:T(8,128)(2,1)S(1)}, bf16[4,400,128]{2,1,0:T(8,128)(2,1)S(1)}) custom-call(s32[1]{0:T(128)} %bitcast.refs_0_.at, bf16[512,128]{1,0:T(8,128)(2,1)S(1)} %get-tuple-element.52.refs_1_, bf16[128,512]{1,0:T(8,128)(2,1)S(1)} %get-tuple-element.53.refs_2_, bf16[256,24576]{1,0:T(8,128)(2,1)} %refs_3_.5, ...), custom_call_target="tpu_custom_call" | custom-call | flops 805306368 | bytes 5505024 | tf_op jit(solution)/shard_map/pallas_call | solution.py:341
  61.4 1.9 %collective-permute-start.22 = (bf16[4,400,128]{2,1,0:T(8,128)(2,1)S(1)}, bf16[4,400,128]{2,1,0:T(8,128)(2,1)S(1)}, u32[]{:S(2)}, u32[]{:S(2)}) collective-permute-start(bf16[4,400,128]{2,1,0:T(8,128)(2,1)S(1)} %get-tuple-element.54), channel_id=1, source_target_pairs={{0,8},{4,36},{8,16},{12,44},{16,24},{20,52},{24,0},{28,60},{32,40}... | collective-permute-start | bytes 1228808 | tf_op jit(solution)/shard_map/ppermute | solution.py:399
  63.5 1.7 %collective-permute-done.19.refs_7_ = bf16[4,400,128]{2,1,0:T(8,128)(2,1)S(1)} collective-permute-done((bf16[4,400,128]{2,1,0:T(8,128)(2,1)S(1)}, bf16[4,400,128]{2,1,0:T(8,128)(2,1)S(1)}, u32[]{:S(2)}, u32[]{:S(2)}) %collective-permute-start.19) | collective-permute-done | bytes 409632 | tf_op jit(solution)/shard_map/ppermute | solution.py:399
  65.2 3.9 %shard_map.75 = (bf16[4,400,128]{2,1,0:T(8,128)(2,1)S(1)}, bf16[4,400,128]{2,1,0:T(8,128)(2,1)S(1)}) custom-call(s32[1]{0:T(128)} %bitcast.refs_0_.at, bf16[512,128]{1,0:T(8,128)(2,1)S(1)} %get-tuple-element.52.refs_1_, bf16[128,512]{1,0:T(8,128)(2,1)S(1)} %get-tuple-element.53.refs_2_, bf16[256,24576]{1,0:T(8,128)(2,1)} %refs_3_.5, ...), custom_call_target="tpu_custom_call" | custom-call | flops 805306368 | bytes 5505024 | tf_op jit(solution)/shard_map/pallas_call | solution.py:341
  69.1 1.4 %collective-permute-start.20 = (bf16[4,400,128]{2,1,0:T(8,128)(2,1)S(1)}, bf16[4,400,128]{2,1,0:T(8,128)(2,1)S(1)}, u32[]{:S(2)}, u32[]{:S(2)}) collective-permute-start(bf16[4,400,128]{2,1,0:T(8,128)(2,1)S(1)} %get-tuple-element.57), channel_id=1, source_target_pairs={{0,8},{4,36},{8,16},{12,44},{16,24},{20,52},{24,0},{28,60},{32,40}... | collective-permute-start | bytes 1228808 | tf_op jit(solution)/shard_map/ppermute | solution.py:399
  71.2 3.5 %shard_map.76 = (f32[4,384,128]{2,1,0:T(8,128)S(1)}, f32[4,384,128]{2,1,0:T(8,128)S(1)}) custom-call(s32[1]{0:T(128)} %bitcast.refs_0_.at, bf16[512,128]{1,0:T(8,128)(2,1)S(1)} %get-tuple-element.52.refs_1_, bf16[128,512]{1,0:T(8,128)(2,1)S(1)} %get-tuple-element.53.refs_2_, bf16[256,24576]{1,0:T(8,128)(2,1)} %refs_3_.5, bf16[16,256,768]{2,1,0:T(8,128)(2,1)S(1)} %bitcast.2, ...), custom_call_target="tpu_custom_call" | custom-call | flops 805306368 | bytes 5505024 | tf_op jit(solution)/shard_map/pallas_call | solution.py:341
  74.8 2.3 %collective-permute-done.20.refs_1_ = bf16[4,400,128]{2,1,0:T(8,128)(2,1)S(1)} collective-permute-done((bf16[4,400,128]{2,1,0:T(8,128)(2,1)S(1)}, bf16[4,400,128]{2,1,0:T(8,128)(2,1)S(1)}, u32[]{:S(2)}, u32[]{:S(2)}) %collective-permute-start.20) | collective-permute-done | bytes 409632 | tf_op jit(solution)/shard_map/ppermute | solution.py:399
  77.2 2.6 %collective-permute-done.23.refs_5_ = bf16[4,400,128]{2,1,0:T(8,128)(2,1)S(1)} collective-permute-done((bf16[4,400,128]{2,1,0:T(8,128)(2,1)S(1)}, bf16[4,400,128]{2,1,0:T(8,128)(2,1)S(1)}, u32[]{:S(2)}, u32[]{:S(2)}) %collective-permute-start.23) | collective-permute-done | bytes 409632 | tf_op jit(solution)/shard_map/ppermute | solution.py:399
  80.5 1.6 %collective-permute-start.24 = (bf16[1,784,128]{2,1,0:T(8,128)(2,1)S(1)}, bf16[1,784,128]{2,1,0:T(8,128)(2,1)S(1)}, u32[]{:S(2)}, u32[]{:S(2)}) collective-permute-start(bf16[1,784,128]{2,1,0:T(8,128)(2,1)S(1)} %get-tuple-element.63), channel_id=1, source_target_pairs={{0,64},{4,20},{8,72},{12,28},{16,80},{20,4},{24,88},{28,12},{32,96... | collective-permute-start | bytes 602120 | tf_op jit(solution)/shard_map/ppermute | solution.py:399
  82.1 1.9 %collective-permute-start.25 = (bf16[1,784,128]{2,1,0:T(8,128)(2,1)S(1)}, bf16[1,784,128]{2,1,0:T(8,128)(2,1)S(1)}, u32[]{:S(2)}, u32[]{:S(2)}) collective-permute-start(bf16[1,784,128]{2,1,0:T(8,128)(2,1)S(1)} %get-tuple-element.64), channel_id=1, source_target_pairs={{0,32},{4,12},{8,40},{12,20},{16,48},{20,28},{24,56},{28,4},{32,64... | collective-permute-start | bytes 602120 | tf_op jit(solution)/shard_map/ppermute | solution.py:399
  84.0 1.4 %collective-permute-start.26 = (bf16[1,784,128]{2,1,0:T(8,128)(2,1)S(1)}, bf16[1,784,128]{2,1,0:T(8,128)(2,1)S(1)}, u32[]{:S(2)}, u32[]{:S(2)}) collective-permute-start(bf16[1,784,128]{2,1,0:T(8,128)(2,1)S(1)} %get-tuple-element.65), channel_id=1, source_target_pairs={{0,96},{4,28},{8,104},{12,4},{16,112},{20,12},{24,120},{28,20},{32... | collective-permute-start | bytes 602120 | tf_op jit(solution)/shard_map/ppermute | solution.py:399
  85.3 2.5 %collective-permute-done.24.two = bf16[1,784,128]{2,1,0:T(8,128)(2,1)S(1)} collective-permute-done((bf16[1,784,128]{2,1,0:T(8,128)(2,1)S(1)}, bf16[1,784,128]{2,1,0:T(8,128)(2,1)S(1)}, u32[]{:S(2)}, u32[]{:S(2)}) %collective-permute-start.24) | collective-permute-done | bytes 200736 | tf_op jit(solution)/shard_map/ppermute | solution.py:399
  87.9 2.1 %collective-permute-done.25.one = bf16[1,784,128]{2,1,0:T(8,128)(2,1)S(1)} collective-permute-done((bf16[1,784,128]{2,1,0:T(8,128)(2,1)S(1)}, bf16[1,784,128]{2,1,0:T(8,128)(2,1)S(1)}, u32[]{:S(2)}, u32[]{:S(2)}) %collective-permute-start.25) | collective-permute-done | bytes 200736 | tf_op jit(solution)/shard_map/ppermute | solution.py:399
  (43 shorter events, 13.3 us)
Async XLA Ops:
  1.5 2.2 %copy-start.1 = (f32[64,128,128]{2,1,0:T(8,128)S(1)}, f32[64,128,128]{2,1,0:T(8,128)}, u32[]{:S(2)}) copy-start(f32[64,128,128]{2,1,0:T(8,128)} %refs_1_.1) | copy-start | bytes 12582916
  10.5 21.1 %collective-permute-start.7 = (bf16[16,256,768]{2,1,0:T(8,128)(2,1)}, bf16[16,256,768]{2,1,0:T(8,128)(2,1)S(1)}, u32[]{:S(2)}, u32[]{:S(2)}) collective-permute-start(bf16[16,256,768]{2,1,0:T(8,128)(2,1)} %get-tuple-element.38), channel_id=1, source_target_pairs={{0,4},{4,0},{8,12},{12,8},{16,20},{20,16},{24,28},{28,24},{32,36},... | collective-permute-start | bytes 18874376 | tf_op jit(solution)/shard_map/ppermute | solution.py:422
  10.6 6.9 %collective-permute-start.2 = (f32[136,128]{1,0:T(8,128)S(1)}, f32[136,128]{1,0:T(8,128)S(1)}, u32[]{:S(2)}, u32[]{:S(2)}) collective-permute-start(f32[136,128]{1,0:T(8,128)S(1)} %get-tuple-element.34.refs_1_), channel_id=1, source_target_pairs={{0,1},{1,2},{2,3},{3,0},{4,5},{5,6},{6,7},{7,4},{8,9},{9,10},{10,1... | collective-permute-start | bytes 208904 | tf_op jit(solution)/shard_map/ppermute | solution.py:266
  12.6 7.6 %collective-permute-start.1 = (f32[136,128]{1,0:T(8,128)S(1)}, f32[136,128]{1,0:T(8,128)S(1)}, u32[]{:S(2)}, u32[]{:S(2)}) collective-permute-start(f32[136,128]{1,0:T(8,128)S(1)} %get-tuple-element.34.refs_1_), channel_id=1, source_target_pairs={{0,2},{1,3},{2,0},{3,1},{4,6},{5,7},{6,4},{7,5},{8,10},{9,11},{10,... | collective-permute-start | bytes 208904 | tf_op jit(solution)/shard_map/ppermute | solution.py:266
  16.2 4.3 %collective-permute-start = (f32[136,128]{1,0:T(8,128)S(1)}, f32[136,128]{1,0:T(8,128)S(1)}, u32[]{:S(2)}, u32[]{:S(2)}) collective-permute-start(f32[136,128]{1,0:T(8,128)S(1)} %get-tuple-element.34.refs_1_), channel_id=1, source_target_pairs={{0,3},{1,0},{2,1},{3,2},{4,7},{5,4},{6,5},{7,6},{8,11},{9,8},{10,9... | collective-permute-start | bytes 208904 | tf_op jit(solution)/shard_map/ppermute | solution.py:266
  21.1 1.3 %collective-permute-start.3 = (f32[136,128]{1,0:T(8,128)S(1)}, f32[136,128]{1,0:T(8,128)S(1)}, u32[]{:S(2)}, u32[]{:S(2)}) collective-permute-start(f32[136,128]{1,0:T(8,128)S(1)} %get-tuple-element.35.refs_1_), channel_id=1, source_target_pairs={{0,4},{4,0},{8,12},{12,8},{16,20},{20,16},{24,28},{28,24},{32,36},... | collective-permute-start | bytes 208904 | tf_op jit(solution)/shard_map/ppermute | solution.py:266
  22.6 5.1 %collective-permute-start.6 = (f32[136,128]{1,0:T(8,128)S(1)}, f32[136,128]{1,0:T(8,128)S(1)}, u32[]{:S(2)}, u32[]{:S(2)}) collective-permute-start(f32[136,128]{1,0:T(8,128)S(1)} %get-tuple-element.36.refs_1_), channel_id=1, source_target_pairs={{0,8},{4,12},{8,16},{12,20},{16,24},{20,28},{24,0},{28,4},{32,40},... | collective-permute-start | bytes 208904 | tf_op jit(solution)/shard_map/ppermute | solution.py:266
  23.2 5.8 %collective-permute-start.5 = (f32[136,128]{1,0:T(8,128)S(1)}, f32[136,128]{1,0:T(8,128)S(1)}, u32[]{:S(2)}, u32[]{:S(2)}) collective-permute-start(f32[136,128]{1,0:T(8,128)S(1)} %get-tuple-element.36.refs_1_), channel_id=1, source_target_pairs={{0,16},{4,20},{8,24},{12,28},{16,0},{20,4},{24,8},{28,12},{32,48},... | collective-permute-start | bytes 208904 | tf_op jit(solution)/shard_map/ppermute | solution.py:266
  25.6 5.5 %collective-permute-start.4 = (f32[136,128]{1,0:T(8,128)S(1)}, f32[136,128]{1,0:T(8,128)S(1)}, u32[]{:S(2)}, u32[]{:S(2)}) collective-permute-start(f32[136,128]{1,0:T(8,128)S(1)} %get-tuple-element.36.refs_1_), channel_id=1, source_target_pairs={{0,24},{4,28},{8,0},{12,4},{16,8},{20,12},{24,16},{28,20},{32,56},... | collective-permute-start | bytes 208904 | tf_op jit(solution)/shard_map/ppermute | solution.py:266
  31.7 19.5 %copy-start = (bf16[16,256,768]{2,1,0:T(8,128)(2,1)}, bf16[16,256,768]{2,1,0:T(8,128)(2,1)S(1)}, u32[]{:S(2)}) copy-start(bf16[16,256,768]{2,1,0:T(8,128)(2,1)S(1)} %collective-permute-done.7.refs_10_.refs_4_) | copy-start | bytes 18874372
  31.7 5.9 %collective-permute-start.10 = (f32[136,128]{1,0:T(8,128)S(1)}, f32[136,128]{1,0:T(8,128)S(1)}, u32[]{:S(2)}, u32[]{:S(2)}) collective-permute-start(f32[136,128]{1,0:T(8,128)S(1)} %get-tuple-element.39.refs_0_), channel_id=1, source_target_pairs={{0,32},{4,36},{8,40},{12,44},{16,48},{20,52},{24,56},{28,60},{32,6... | collective-permute-start | bytes 208904 | tf_op jit(solution)/shard_map/ppermute | solution.py:266
  33.3 5.9 %collective-permute-start.9 = (f32[136,128]{1,0:T(8,128)S(1)}, f32[136,128]{1,0:T(8,128)S(1)}, u32[]{:S(2)}, u32[]{:S(2)}) collective-permute-start(f32[136,128]{1,0:T(8,128)S(1)} %get-tuple-element.39.refs_0_), channel_id=1, source_target_pairs={{0,64},{4,68},{8,72},{12,76},{16,80},{20,84},{24,88},{28,92},{32,9... | collective-permute-start | bytes 208904 | tf_op jit(solution)/shard_map/ppermute | solution.py:266
  36.2 4.3 %collective-permute-start.8 = (f32[136,128]{1,0:T(8,128)S(1)}, f32[136,128]{1,0:T(8,128)S(1)}, u32[]{:S(2)}, u32[]{:S(2)}) collective-permute-start(f32[136,128]{1,0:T(8,128)S(1)} %get-tuple-element.39.refs_0_), channel_id=1, source_target_pairs={{0,96},{4,100},{8,104},{12,108},{16,112},{20,116},{24,120},{28,124... | collective-permute-start | bytes 208904 | tf_op jit(solution)/shard_map/ppermute | solution.py:266
  42.3 5.0 %collective-permute-start.13 = (bf16[64,128]{1,0:T(8,128)(2,1)S(1)}, bf16[64,128]{1,0:T(8,128)(2,1)S(1)}, u32[]{:S(2)}, u32[]{:S(2)}) collective-permute-start(bf16[64,128]{1,0:T(8,128)(2,1)S(1)} %get-tuple-element.47.refs_1_), channel_id=1, source_target_pairs={{0,1},{1,2},{2,3},{3,0},{4,5},{5,6},{6,7},{7,4},{8,9},{9,10},{10,1... | collective-permute-start | bytes 49160 | tf_op jit(solution)/shard_map/ppermute | solution.py:266
  43.1 5.2 %collective-permute-start.12 = (bf16[64,128]{1,0:T(8,128)(2,1)S(1)}, bf16[64,128]{1,0:T(8,128)(2,1)S(1)}, u32[]{:S(2)}, u32[]{:S(2)}) collective-permute-start(bf16[64,128]{1,0:T(8,128)(2,1)S(1)} %get-tuple-element.47.refs_1_), channel_id=1, source_target_pairs={{0,2},{1,3},{2,0},{3,1},{4,6},{5,7},{6,4},{7,5},{8,10},{9,11},{10,... | collective-permute-start | bytes 49160 | tf_op jit(solution)/shard_map/ppermute | solution.py:266
  46.2 3.7 %collective-permute-start.11 = (bf16[64,128]{1,0:T(8,128)(2,1)S(1)}, bf16[64,128]{1,0:T(8,128)(2,1)S(1)}, u32[]{:S(2)}, u32[]{:S(2)}) collective-permute-start(bf16[64,128]{1,0:T(8,128)(2,1)S(1)} %get-tuple-element.47.refs_1_), channel_id=1, source_target_pairs={{0,3},{1,0},{2,1},{3,2},{4,7},{5,4},{6,5},{7,6},{8,11},{9,8},{10,9... | collective-permute-start | bytes 49160 | tf_op jit(solution)/shard_map/ppermute | solution.py:266
  47.3 2.7 %collective-permute-start.14 = (bf16[64,128]{1,0:T(8,128)(2,1)S(1)}, bf16[64,128]{1,0:T(8,128)(2,1)S(1)}, u32[]{:S(2)}, u32[]{:S(2)}) collective-permute-start(bf16[64,128]{1,0:T(8,128)(2,1)S(1)} %get-tuple-element.47.refs_1_), channel_id=1, source_target_pairs={{0,4},{4,0},{8,12},{12,8},{16,20},{20,16},{24,28},{28,24},{32,36},... | collective-permute-start | bytes 49160 | tf_op jit(solution)/shard_map/ppermute | solution.py:422
  47.3 2.7 %collective-permute-start.17 = (bf16[64,128]{1,0:T(8,128)(2,1)S(1)}, bf16[64,128]{1,0:T(8,128)(2,1)S(1)}, u32[]{:S(2)}, u32[]{:S(2)}) collective-permute-start(bf16[64,128]{1,0:T(8,128)(2,1)S(1)} %collective-permute-done.13.refs_4_), channel_id=1, source_target_pairs={{0,4},{4,0},{8,12},{12,8},{16,20},{20,16},{24,28},{28,24},{32,36},... | collective-permute-start | bytes 49160 | tf_op jit(solution)/shard_map/ppermute | solution.py:422
  48.3 1.7 %collective-permute-start.16 = (bf16[64,128]{1,0:T(8,128)(2,1)S(1)}, bf16[64,128]{1,0:T(8,128)(2,1)S(1)}, u32[]{:S(2)}, u32[]{:S(2)}) collective-permute-start(bf16[64,128]{1,0:T(8,128)(2,1)S(1)} %collective-permute-done.12.refs_3_), channel_id=1, source_target_pairs={{0,4},{4,0},{8,12},{12,8},{16,20},{20,16},{24,28},{28,24},{32,36},... | collective-permute-start | bytes 49160 | tf_op jit(solution)/shard_map/ppermute | solution.py:422
  50.0 1.2 %collective-permute-start.15 = (bf16[64,128]{1,0:T(8,128)(2,1)S(1)}, bf16[64,128]{1,0:T(8,128)(2,1)S(1)}, u32[]{:S(2)}, u32[]{:S(2)}) collective-permute-start(bf16[64,128]{1,0:T(8,128)(2,1)S(1)} %collective-permute-done.11.refs_2_), channel_id=1, source_target_pairs={{0,4},{4,0},{8,12},{12,8},{16,20},{20,16},{24,28},{28,24},{32,36},... | collective-permute-start | bytes 49160 | tf_op jit(solution)/shard_map/ppermute | solution.py:422
  55.2 8.3 %collective-permute-start.18 = (bf16[4,400,128]{2,1,0:T(8,128)(2,1)S(1)}, bf16[4,400,128]{2,1,0:T(8,128)(2,1)S(1)}, u32[]{:S(2)}, u32[]{:S(2)}) collective-permute-start(bf16[4,400,128]{2,1,0:T(8,128)(2,1)S(1)} %get-tuple-element.49), channel_id=1, source_target_pairs={{0,8},{4,36},{8,16},{12,44},{16,24},{20,52},{24,0},{28,60},{32,40}... | collective-permute-start | bytes 1228808 | tf_op jit(solution)/shard_map/ppermute | solution.py:399
  56.0 9.2 %collective-permute-start.19 = (bf16[4,400,128]{2,1,0:T(8,128)(2,1)S(1)}, bf16[4,400,128]{2,1,0:T(8,128)(2,1)S(1)}, u32[]{:S(2)}, u32[]{:S(2)}) collective-permute-start(bf16[4,400,128]{2,1,0:T(8,128)(2,1)S(1)} %get-tuple-element.50), channel_id=1, source_target_pairs={{0,24},{4,100},{8,0},{12,108},{16,8},{20,116},{24,16},{28,124},{32... | collective-permute-start | bytes 1228808 | tf_op jit(solution)/shard_map/ppermute | solution.py:399
  61.4 13.4 %collective-permute-start.22 = (bf16[4,400,128]{2,1,0:T(8,128)(2,1)S(1)}, bf16[4,400,128]{2,1,0:T(8,128)(2,1)S(1)}, u32[]{:S(2)}, u32[]{:S(2)}) collective-permute-start(bf16[4,400,128]{2,1,0:T(8,128)(2,1)S(1)} %get-tuple-element.54), channel_id=1, source_target_pairs={{0,8},{4,36},{8,16},{12,44},{16,24},{20,52},{24,0},{28,60},{32,40}... | collective-permute-start | bytes 1228808 | tf_op jit(solution)/shard_map/ppermute | solution.py:399
  63.3 7.9 %slice-start = ((s8[6291456]{0:T(1024)(128)(4,1)}), s8[4194304]{0:T(1024)(128)(4,1)S(1)}, s32[]{:S(2)}) async-start(s8[6291456]{0:T(1024)(128)(4,1)} %bitcast.1), calls=%async_computation | async-start | bytes 8388608
  63.3 7.9 %slice-start.1 = ((s8[6291456]{0:T(1024)(128)(4,1)}), s8[2097152]{0:T(1024)(128)(4,1)S(1)}, s32[]{:S(2)}) async-start(s8[6291456]{0:T(1024)(128)(4,1)} %bitcast.1), calls=%async_computation.1 | async-start | bytes 4194304
  63.3 11.5 %collective-permute-start.21 = (bf16[4,400,128]{2,1,0:T(8,128)(2,1)S(1)}, bf16[4,400,128]{2,1,0:T(8,128)(2,1)S(1)}, u32[]{:S(2)}, u32[]{:S(2)}) collective-permute-start(bf16[4,400,128]{2,1,0:T(8,128)(2,1)S(1)} %get-tuple-element.55), channel_id=1, source_target_pairs={{0,24},{4,100},{8,0},{12,108},{16,8},{20,116},{24,16},{28,124},{32... | collective-permute-start | bytes 1228808 | tf_op jit(solution)/shard_map/ppermute | solution.py:399
  69.1 8.0 %collective-permute-start.20 = (bf16[4,400,128]{2,1,0:T(8,128)(2,1)S(1)}, bf16[4,400,128]{2,1,0:T(8,128)(2,1)S(1)}, u32[]{:S(2)}, u32[]{:S(2)}) collective-permute-start(bf16[4,400,128]{2,1,0:T(8,128)(2,1)S(1)} %get-tuple-element.57), channel_id=1, source_target_pairs={{0,8},{4,36},{8,16},{12,44},{16,24},{20,52},{24,0},{28,60},{32,40}... | collective-permute-start | bytes 1228808 | tf_op jit(solution)/shard_map/ppermute | solution.py:399
  70.6 9.2 %collective-permute-start.23 = (bf16[4,400,128]{2,1,0:T(8,128)(2,1)S(1)}, bf16[4,400,128]{2,1,0:T(8,128)(2,1)S(1)}, u32[]{:S(2)}, u32[]{:S(2)}) collective-permute-start(bf16[4,400,128]{2,1,0:T(8,128)(2,1)S(1)} %get-tuple-element.58), channel_id=1, source_target_pairs={{0,24},{4,100},{8,0},{12,108},{16,8},{20,116},{24,16},{28,124},{32... | collective-permute-start | bytes 1228808 | tf_op jit(solution)/shard_map/ppermute | solution.py:399
  80.5 7.4 %collective-permute-start.24 = (bf16[1,784,128]{2,1,0:T(8,128)(2,1)S(1)}, bf16[1,784,128]{2,1,0:T(8,128)(2,1)S(1)}, u32[]{:S(2)}, u32[]{:S(2)}) collective-permute-start(bf16[1,784,128]{2,1,0:T(8,128)(2,1)S(1)} %get-tuple-element.63), channel_id=1, source_target_pairs={{0,64},{4,20},{8,72},{12,28},{16,80},{20,4},{24,88},{28,12},{32,96... | collective-permute-start | bytes 602120 | tf_op jit(solution)/shard_map/ppermute | solution.py:399
  82.1 7.8 %collective-permute-start.25 = (bf16[1,784,128]{2,1,0:T(8,128)(2,1)S(1)}, bf16[1,784,128]{2,1,0:T(8,128)(2,1)S(1)}, u32[]{:S(2)}, u32[]{:S(2)}) collective-permute-start(bf16[1,784,128]{2,1,0:T(8,128)(2,1)S(1)} %get-tuple-element.64), channel_id=1, source_target_pairs={{0,32},{4,12},{8,40},{12,20},{16,48},{20,28},{24,56},{28,4},{32,64... | collective-permute-start | bytes 602120 | tf_op jit(solution)/shard_map/ppermute | solution.py:399
  84.0 6.0 %collective-permute-start.26 = (bf16[1,784,128]{2,1,0:T(8,128)(2,1)S(1)}, bf16[1,784,128]{2,1,0:T(8,128)(2,1)S(1)}, u32[]{:S(2)}, u32[]{:S(2)}) collective-permute-start(bf16[1,784,128]{2,1,0:T(8,128)(2,1)S(1)} %get-tuple-element.65), channel_id=1, source_target_pairs={{0,96},{4,28},{8,104},{12,4},{16,112},{20,12},{24,120},{28,20},{32... | collective-permute-start | bytes 602120 | tf_op jit(solution)/shard_map/ppermute | solution.py:399
